TPU v7x, 768 devices: a whole 4x8x12 slice. The times are simulated.
768 devices in a mesh: blk: 96 (over z_lo, y, x), sub: 8 (over z_hi, core).
Axes of the slice: x: 4, y: 8, z: 12 (z_hi: 4, z_lo: 3; z = z_hi * 3 + z_lo), core: 2. Of those that a mesh axis runs over, the one named last changes fastest.
Arguments:
- image: bfloat16 [393216, 768], P(('blk', 'sub')), may hold values from -0.21582031 to 0.21582031
- text: bfloat16 [393216, 768], P(('blk', 'sub')), may hold values from -0.21582031 to 0.21582031
- scale: float32 [1], replicated, may hold values from 5 to 20
- shift: float32 [1], replicated, may hold values from -6 to -1
Outputs:
- row_loss: float32 [393216], P(('blk', 'sub'))
- image_grad: float32 [393216, 768], P(('blk', 'sub'))
- text_grad: float32 [393216, 768], P(('blk', 'sub'))
All inputs are finite; a program needn't handle non-finite values.
Results may differ from a plain program's by a relative error of at most 0.0036.
Values may be sent and summed in bfloat16 or wider, within the bound.
No kernel may reach another device: no remote copies, remote signals or barrier semaphores. Data moves between devices by JAX's collectives and lax.ppermute only.
A program may use at most 32 MiB of HBM per device.

v0:
```python
import jax
import jax.numpy as jnp
from jax import lax
from jax.sharding import PartitionSpec as P

EPS = 1e-06


def shifted(array, axis, by):
    devices = lax.axis_size(axis)
    return lax.ppermute(array, axis, [(i, (i + by) % devices) for i in range(devices)])


def normalize(values):
    full = values.astype(jnp.float32)
    length = jnp.sqrt(jnp.sum(full * full, axis=-1, keepdims=True) + EPS)
    return (full / length, length)


def unit_back(grad, unit, length):
    return (grad - unit * jnp.sum(unit * grad, axis=-1, keepdims=True)) / length


def body(image, text, scale, shift):
    image_unit, image_norm = normalize(image)
    text_unit, text_norm = normalize(text)
    image_low = image_unit.astype(jnp.bfloat16)
    text_low = text_unit.astype(jnp.bfloat16)
    rows = image.shape[0]
    temper = scale[0]
    offset = shift[0]
    diagonal = jnp.eye(rows, dtype=jnp.float32)
    loss = jnp.zeros((rows,), jnp.float32)
    grad_here = jnp.zeros(image_unit.shape, jnp.float32)
    carried = None
    current = text_low
    for turn in range(3):
        if turn > 0:
            current = shifted(current, ("blk", "sub"), 1)
        logits = (
            temper
            * lax.dot_general(
                image_low, current, (((1,), (1,)), ((), ())), preferred_element_type=jnp.float32
            )
            + offset
        )
        sign = 2.0 * diagonal - 1.0 if turn == 0 else -1.0
        loss = loss + jnp.sum(jax.nn.softplus(-sign * logits), axis=1)
        coef = (-sign * jax.nn.sigmoid(-sign * logits)).astype(jnp.bfloat16)
        grad_here = grad_here + temper * jnp.dot(coef, current, preferred_element_type=jnp.float32)
        piece = temper * lax.dot_general(
            coef, image_low, (((0,), (0,)), ((), ())), preferred_element_type=jnp.float32
        )
        if turn == 0:
            carried = piece
        else:
            carried = shifted(carried, ("blk", "sub"), 1) + piece
    unit_text_grad = shifted(carried, ("blk", "sub"), -2)
    row_loss = loss / rows
    image_grad = unit_back(grad_here, image_unit, image_norm)
    text_grad = unit_back(unit_text_grad, text_unit, text_norm)
    return (row_loss, image_grad, text_grad)


def solution(mesh):
    in_specs = (P(("blk", "sub"), None), P(("blk", "sub"), None), P(), P())
    out_specs = (P(("blk", "sub")), P(("blk", "sub"), None), P(("blk", "sub"), None))
    return jax.shard_map(body, mesh=mesh, in_specs=in_specs, out_specs=out_specs, check_vma=False)
```

profile of v0, /device:TPU:64, one launch (start us, length us, event | category | flops | bytes accessed | tf_op | source)
XLA Modules:
  0.0 290.6 jit_solution(3664522350779965814)
XLA Ops:
  0.6 0.0 copy-start
  2.0 0.0 copy-start.1
  2.0 1.4 fusion.1
  3.5 1.4 fusion
  4.8 0.0 copy-done
  4.9 0.2 fusion.10
  5.1 0.0 copy-done.1
  5.1 1.3 fusion.6
  6.4 0.8 convolution_multiply_fusion
  7.2 1.9 collective-permute-start.2
  9.2 9.2 %collective-permute-start = (bf16[512,768]{1,0:T(8,128)(2,1)S(1)}, bf16[512,768]{1,0:T(8,128)(2,1)S(1)}, u32[]{:S(2)}, u32[]{:S(2)}) collective-permute-start(bf16[512,768]{1,0:T(8,128)(2,1)S(1)} %fusion.10), channel_id=1, source_target_pairs={{0,1},{1,2},{2,3},{3,4},{4,5},{5,6},{6,7},{7,8},{8,9},{9,10},{10,1... | collective-permute-start | bytes 2359304 | tf_op jit(solution)/shard_map/ppermute | solution.py:11
  18.4 81.1 %collective-permute-done = bf16[512,768]{1,0:T(8,128)(2,1)S(1)} collective-permute-done((bf16[512,768]{1,0:T(8,128)(2,1)S(1)}, bf16[512,768]{1,0:T(8,128)(2,1)S(1)}, u32[]{:S(2)}, u32[]{:S(2)}) %collective-permute-start) | collective-permute-done | bytes 786464 | tf_op jit(solution)/shard_map/ppermute | solution.py:11
  99.5 1.9 collective-permute-start.1
  101.4 1.2 fusion.7
  102.7 0.0 collective-permute-done.2
  102.7 0.8 multiply_add_fusion.1
  103.5 1.9 collective-permute-start.3
  105.5 0.6 fusion.13
  106.1 34.0 %collective-permute-done.1 = bf16[512,768]{1,0:T(8,128)(2,1)S(1)} collective-permute-done((bf16[512,768]{1,0:T(8,128)(2,1)S(1)}, bf16[512,768]{1,0:T(8,128)(2,1)S(1)}, u32[]{:S(2)}, u32[]{:S(2)}) %collective-permute-start.1) | collective-permute-done | bytes 786464 | tf_op jit(solution)/shard_map/ppermute | solution.py:11
  140.1 1.2 fusion.8
  141.4 0.8 fusion.12
  142.2 43.4 %collective-permute-done.3 = f32[512,768]{1,0:T(8,128)S(1)} collective-permute-done((f32[512,768]{1,0:T(8,128)S(1)}, f32[512,768]{1,0:T(8,128)S(1)}, u32[]{:S(2)}, u32[]{:S(2)}) %collective-permute-start.3) | collective-permute-done | bytes 1572896 | tf_op jit(solution)/shard_map/ppermute | solution.py:11
  185.6 0.2 multiply_add_fusion
  185.8 4.9 %collective-permute-start.4 = (f32[512,768]{1,0:T(8,128)S(1)}, f32[512,768]{1,0:T(8,128)S(1)}, u32[]{:S(2)}, u32[]{:S(2)}) collective-permute-start(f32[512,768]{1,0:T(8,128)S(1)} %multiply_add_fusion), channel_id=1, source_target_pairs={{0,766},{1,767},{2,0},{3,1},{4,2},{5,3},{6,4},{7,5},{8,6},{9,7},{1... | collective-permute-start | bytes 4718600 | tf_op jit(solution)/shard_map/ppermute | solution.py:11
  190.8 0.6 fusion.11
  191.4 0.6 add_multiply_fusion.1
  192.0 0.9 multiply_reduce_fusion.1
  192.9 1.5 subtract_divide_fusion.1
  194.4 94.4 %collective-permute-done.4 = f32[512,768]{1,0:T(8,128)S(1)} collective-permute-done((f32[512,768]{1,0:T(8,128)S(1)}, f32[512,768]{1,0:T(8,128)S(1)}, u32[]{:S(2)}, u32[]{:S(2)}) %collective-permute-start.4) | collective-permute-done | bytes 1572896 | tf_op jit(solution)/shard_map/ppermute | solution.py:11
  288.8 0.4 multiply_reduce_fusion
  289.1 1.5 subtract_divide_fusion
  (2 shorter events, 0.0 us)
Async XLA Ops:
  0.6 4.2 %copy-start = (bf16[512,768]{1,0:T(8,128)(2,1)S(1)}, bf16[512,768]{1,0:T(8,128)(2,1)}, u32[]{:S(2)}) copy-start(bf16[512,768]{1,0:T(8,128)(2,1)} %param.5) | copy-start | bytes 2359300
  2.0 3.1 %copy-start.1 = (bf16[512,768]{1,0:T(8,128)(2,1)S(1)}, bf16[512,768]{1,0:T(8,128)(2,1)}, u32[]{:S(2)}) copy-start(bf16[512,768]{1,0:T(8,128)(2,1)} %param.4) | copy-start | bytes 2359300
  7.2 95.4 %collective-permute-start.2 = (f32[512,768]{1,0:T(8,128)S(1)}, f32[512,768]{1,0:T(8,128)S(1)}, u32[]{:S(2)}, u32[]{:S(2)}) collective-permute-start(f32[512,768]{1,0:T(8,128)S(1)} %convolution_multiply_fusion), channel_id=1, source_target_pairs={{0,1},{1,2},{2,3},{3,4},{4,5},{5,6},{6,7},{7,8},{8,9},{9,10},{10,1... | collective-permute-start | bytes 4718600 | tf_op jit(solution)/shard_map/ppermute | solution.py:11
  9.2 90.3 %collective-permute-start = (bf16[512,768]{1,0:T(8,128)(2,1)S(1)}, bf16[512,768]{1,0:T(8,128)(2,1)S(1)}, u32[]{:S(2)}, u32[]{:S(2)}) collective-permute-start(bf16[512,768]{1,0:T(8,128)(2,1)S(1)} %fusion.10), channel_id=1, source_target_pairs={{0,1},{1,2},{2,3},{3,4},{4,5},{5,6},{6,7},{7,8},{8,9},{9,10},{10,1... | collective-permute-start | bytes 2359304 | tf_op jit(solution)/shard_map/ppermute | solution.py:11
  99.5 40.6 %collective-permute-start.1 = (bf16[512,768]{1,0:T(8,128)(2,1)S(1)}, bf16[512,768]{1,0:T(8,128)(2,1)S(1)}, u32[]{:S(2)}, u32[]{:S(2)}) collective-permute-start(bf16[512,768]{1,0:T(8,128)(2,1)S(1)} %collective-permute-done), channel_id=1, source_target_pairs={{0,1},{1,2},{2,3},{3,4},{4,5},{5,6},{6,7},{7,8},{8,9},{9,10},{10,1... | collective-permute-start | bytes 2359304 | tf_op jit(solution)/shard_map/ppermute | solution.py:11
  103.5 82.1 %collective-permute-start.3 = (f32[512,768]{1,0:T(8,128)S(1)}, f32[512,768]{1,0:T(8,128)S(1)}, u32[]{:S(2)}, u32[]{:S(2)}) collective-permute-start(f32[512,768]{1,0:T(8,128)S(1)} %multiply_add_fusion.1), channel_id=1, source_target_pairs={{0,1},{1,2},{2,3},{3,4},{4,5},{5,6},{6,7},{7,8},{8,9},{9,10},{10,1... | collective-permute-start | bytes 4718600 | tf_op jit(solution)/shard_map/ppermute | solution.py:11
  185.8 103.0 %collective-permute-start.4 = (f32[512,768]{1,0:T(8,128)S(1)}, f32[512,768]{1,0:T(8,128)S(1)}, u32[]{:S(2)}, u32[]{:S(2)}) collective-permute-start(f32[512,768]{1,0:T(8,128)S(1)} %multiply_add_fusion), channel_id=1, source_target_pairs={{0,766},{1,767},{2,0},{3,1},{4,2},{5,3},{6,4},{7,5},{8,6},{9,7},{1... | collective-permute-start | bytes 4718600 | tf_op jit(solution)/shard_map/ppermute | solution.py:11
where the time goes:
time: 291 us
  waiting for transfers between devices  253 us (87%)
  starting transfers between devices  19.9 us (7%)
  matrix products  8.46 us (3%)
  other arithmetic  7.19 us (2%)
    ppermute x5, waiting for transfers between devices, shifted(): lax.ppermute(array, axis, [(i, (i + by) % devices) for i in range(devices)])  253 us
    ppermute x5, starting transfers between devices, shifted(): lax.ppermute(array, axis, [(i, (i + by) % devices) for i in range(devices)])  19.9 us
  transfers between devices with their start and end apart: 5, of which 4 were waited for; matrix products, arithmetic and copies ran while one was open for 3% of the time, Pallas kernels for 0%

commit v1 on v0

v1 whole, which is shorter than its diff:
```python
import jax
import jax.numpy as jnp
from jax import lax
from jax.experimental import pallas as pl
from jax.experimental.pallas import tpu as pltpu
from jax.sharding import PartitionSpec as P

EPS = 1e-06
AXES = ("blk", "sub")
TILE = 256
F32 = jnp.float32
BF16 = jnp.bfloat16
VMEM = pl.BlockSpec(memory_space=pltpu.VMEM)
SMEM = pl.BlockSpec(memory_space=pltpu.SMEM)
ANY = pl.BlockSpec(memory_space=pl.ANY)
PARAMS = pltpu.CompilerParams(vmem_limit_bytes=16 * 2**20)


def exchange(array, odd_by, even_by):
    count = lax.axis_size(AXES)
    steps = [(i, odd_by if i % 2 else even_by) for i in range(count)]
    return lax.ppermute(array, AXES, [(i, (i + by) % count) for i, by in steps if by is not None])


def exchange_in_parts(array, parts, odd_by, even_by):
    size = array.shape[0] // parts
    return [
        exchange(lax.slice_in_dim(array, at, at + size), odd_by, even_by)
        for at in range(0, array.shape[0], size)
    ]


def is_odd():
    return lax.rem(lax.axis_index("sub"), 2) == 1


def select(odd, one, other, at):
    return jnp.where(odd, one[at, :].astype(F32), other[at, :].astype(F32))


def inverse_norm(full):
    return lax.rsqrt(jnp.sum(full * full, axis=-1, keepdims=True) + EPS)


def products(own, other, temper, offset):
    return temper * lax.dot_general(
        own, other, (((1,), (1,)), ((), ())), preferred_element_type=F32
    ) + offset


def terms(logits, diagonal=None):
    if diagonal is not None:
        logits = jnp.where(diagonal, -logits, logits)
    power = jnp.exp(logits)
    above = 1.0 + power
    plus = jnp.where(
        power < 0.01, power * (1.0 - power * (0.5 - power * (1.0 / 3.0))), jnp.log(above)
    )
    coef = power / above
    if diagonal is not None:
        coef = jnp.where(diagonal, -coef, coef)
    return coef.astype(BF16), jnp.sum(plus, axis=1, keepdims=True)


def weighted(coef, other):
    return jnp.dot(coef, other, preferred_element_type=F32)


def on_diagonal(start, rows, columns):
    row = lax.broadcasted_iota(jnp.int32, (rows, columns), 0) + start
    return row == lax.broadcasted_iota(jnp.int32, (rows, columns), 1)


def finished(acc, raw, inverse, temper):
    grad = temper * acc
    unit = raw * inverse
    return (grad - unit * jnp.sum(unit * grad, axis=-1, keepdims=True)) * inverse


def put(grad, odd, image_grad, text_grad, sems, number, act):
    at = pl.ds(number * TILE, TILE)

    @pl.when(odd)
    def _():
        act(pltpu.make_async_copy(grad.at[at, :], image_grad.at[at, :], sems.at[number]))

    @pl.when(jnp.logical_not(odd))
    def _():
        act(pltpu.make_async_copy(grad.at[at, :], text_grad.at[at, :], sems.at[number]))


def prepare_kernel(image, text, xlow, ylow, xinv, yinv):
    odd = is_odd()
    for start in range(0, image.shape[0], TILE):
        at = pl.ds(start, TILE)
        for low, inv, full in (
            (xlow, xinv, select(odd, image, text, at)),
            (ylow, yinv, select(odd, text, image, at)),
        ):
            inverse = inverse_norm(full)
            inv[at, :] = inverse
            low[at, :] = (full * inverse).astype(BF16)


def arrived_kernel(text_piece, image_piece, low):
    odd = is_odd()
    for start in range(0, low.shape[0], TILE):
        at = pl.ds(start, TILE)
        full = select(odd, text_piece, image_piece, at)
        low[at, :] = (full * inverse_norm(full)).astype(BF16)


def local_kernel(scale, shift, xlow, ylow, *refs):
    pieces, (xacc, yacc, xloss, yloss, xsend) = refs[:-5], refs[-5:]
    temper, offset = scale[0], shift[0]
    rows = xlow.shape[0]
    for start in range(0, rows, TILE):
        at = pl.ds(start, TILE)
        xsend[at, :] = xlow[at, :]
        diagonal = on_diagonal(start, TILE, rows)
        coef, plus = terms(products(xlow[at, :], ylow[...], temper, offset), diagonal)
        acc = weighted(coef, ylow[...])
        for piece in pieces:
            coef, more = terms(products(xlow[at, :], piece[...], temper, offset))
            plus += more
            acc += weighted(coef, piece[...])
        xloss[at, :] = plus
        xacc[at, :] = acc
        coef, plus = terms(products(ylow[at, :], xlow[...], temper, offset), diagonal)
        yloss[at, :] = plus
        yacc[at, :] = weighted(coef, xlow[...])


def first_kernel(
    scale, shift, image, text, xlow, xinv, xacc, xloss_in, low,
    image_grad, text_grad, xloss, grad, sems,
):
    temper, offset = scale[0], shift[0]
    odd = is_odd()
    count = xlow.shape[0] // TILE
    for number in range(count):
        at = pl.ds(number * TILE, TILE)
        coef, plus = terms(products(xlow[at, :], low[...], temper, offset))
        xloss[at, :] = xloss_in[at, :] + plus
        acc = xacc[at, :] + weighted(coef, low[...])
        grad[at, :] = finished(acc, select(odd, image, text, at), xinv[at, :], temper)
        put(grad, odd, image_grad, text_grad, sems, number, lambda copy: copy.start())
    for number in range(count):
        put(grad, odd, image_grad, text_grad, sems, number, lambda copy: copy.wait())


def second_kernel(scale, shift, ylow, yacc_in, yloss_in, xloss, *refs):
    pieces, (yacc, loss) = refs[:-2], refs[-2:]
    temper, offset = scale[0], shift[0]
    odd = is_odd()
    for start in range(0, ylow.shape[0], TILE):
        at = pl.ds(start, TILE)
        total, acc = yloss_in[at, :], yacc_in[at, :]
        for piece in pieces:
            coef, plus = terms(products(ylow[at, :], piece[...], temper, offset))
            total += plus
            acc += weighted(coef, piece[...])
        loss[at, :] = jnp.where(odd, xloss[at, :], total)
        yacc[at, :] = acc


def last_kernel(
    scale, shift, image, text, ylow, yinv, yacc, loss_in, low, image_in, text_in,
    image_grad, text_grad, loss, grad, sems,
):
    del image_in, text_in
    temper, offset = scale[0], shift[0]
    odd = is_odd()
    rows = ylow.shape[0]
    for number in range(rows // TILE):
        at = pl.ds(number * TILE, TILE)
        coef, plus = terms(products(ylow[at, :], low[...], temper, offset))
        acc = yacc[at, :] + weighted(coef, low[...])
        grad[at, :] = finished(acc, select(odd, text, image, at), yinv[at, :], temper)
        put(grad, jnp.logical_not(odd), image_grad, text_grad, sems, number, lambda copy: copy.start())
        total = loss_in[at, :] + jnp.where(odd, 0.0, plus)
        loss[at] = jnp.sum(total, axis=1) * (1.0 / rows)
    for number in range(rows // TILE):
        put(grad, jnp.logical_not(odd), image_grad, text_grad, sems, number, lambda copy: copy.wait())


def cost():
    return pl.CostEstimate(flops=1, bytes_accessed=1, transcendentals=0)


def body(image, text, scale, shift):
    rows, width = image.shape
    text_piece = exchange(text, 2, None)
    image_piece = exchange(image, None, -2)

    wide = jax.ShapeDtypeStruct((rows, width), F32)
    slim = jax.ShapeDtypeStruct((rows, width), BF16)
    thin = jax.ShapeDtypeStruct((rows, 1), F32)
    grads = [pltpu.VMEM((rows, width), F32), pltpu.SemaphoreType.DMA((rows // TILE,))]

    def call(kernel, name, inputs, outs, **more):
        specs = dict(out_specs=(VMEM,) * len(outs), in_specs=[VMEM] * len(inputs))
        specs.update(more)
        return pl.pallas_call(
            kernel, out_shape=outs, compiler_params=PARAMS, cost_estimate=cost(), name=name, **specs
        )(*inputs)

    numbers = (scale, shift)
    xlow, ylow, xinv, yinv = call(prepare_kernel, "prepare", (image, text), (slim, slim, thin, thin))
    r0 = exchange_in_parts(xlow, 2, -1, 1)
    xacc, yacc, xloss, yloss, xsend = call(
        local_kernel, "local", (*numbers, xlow, ylow, *r0), (wide, wide, thin, thin, slim),
        in_specs=[SMEM] * 2 + [VMEM] * (2 + len(r0)),
    )
    r2 = exchange(xsend, -2, 2)
    (r1,) = call(arrived_kernel, "arrived", (text_piece, image_piece), (slim,))
    r3 = exchange_in_parts(r1, 2, -1, 1)
    image_grad, text_grad, xloss = call(
        first_kernel, "first", (*numbers, image, text, xlow, xinv, xacc, xloss, r1), (wide, wide, thin),
        in_specs=[SMEM] * 2 + [VMEM] * 7, out_specs=(ANY, ANY, VMEM), scratch_shapes=grads,
    )
    yacc, loss = call(
        second_kernel, "second", (*numbers, ylow, yacc, yloss, xloss, *r3), (wide, thin),
        in_specs=[SMEM] * 2 + [VMEM] * (4 + len(r3)),
    )
    image_grad, text_grad, loss = call(
        last_kernel, "last",
        (*numbers, image, text, ylow, yinv, yacc, loss, r2, image_grad, text_grad),
        (wide, wide, jax.ShapeDtypeStruct((rows,), F32)),
        in_specs=[SMEM] * 2 + [VMEM] * 7 + [ANY] * 2, out_specs=(ANY, ANY, VMEM), scratch_shapes=grads,
        input_output_aliases={9: 0, 10: 1},
    )
    return loss, image_grad, text_grad


def solution(mesh):
    in_specs = (P(AXES, None), P(AXES, None), P(), P())
    out_specs = (P(AXES), P(AXES, None), P(AXES, None))
    return jax.shard_map(body, mesh=mesh, in_specs=in_specs, out_specs=out_specs, check_vma=False)
```

time: 291 us -> 77.6 us (0.27)
  the two profiles are of different devices: /device:TPU:64 before, /device:TPU:1 now
where the time goes in v1:
time: 77.6 us; the launch traced here: 77.2 us
  starting transfers between devices  44.8 us (58%)
  waiting for transfers between devices  15.2 us (20%)
  Pallas kernels  12.7 us (16%)
  local copies, waits for them, and re-layouts  2.38 us (3%)
  between operations  2.09 us (3%)
    ppermute x7, starting transfers between devices, exchange(): lax.ppermute(array, AXES, [(i, (i + by) % count) for i, by in steps if by...  44.8 us
    ppermute x7, waiting for transfers between devices, exchange(): lax.ppermute(array, AXES, [(i, (i + by) % count) for i, by in steps if by...  15.2 us
    pallas_call x6, Pallas kernels, call(): pl.pallas_call(kernel, out_shape=outs, compiler_params=PARAMS, cost_estim...  12.7 us
    unnamed x8, local copies, waits for them, and re-layouts  2.27 us
  transfers between devices with their start and end apart: 7, of which 3 were waited for; matrix products, arithmetic and copies ran while one was open for 0% of the time, Pallas kernels for 12%

profile of v1, /device:TPU:1, one launch (start us, length us, event | category | flops | bytes accessed | tf_op | source)
XLA Modules:
  0.0 77.2 jit_solution(7576355829185623353)
XLA Ops:
  0.6 8.4 %collective-permute-start.2 = (bf16[512,768]{1,0:T(8,128)(2,1)}, bf16[512,768]{1,0:T(8,128)(2,1)S(1)}, u32[]{:S(2)}, u32[]{:S(2)}) collective-permute-start(bf16[512,768]{1,0:T(8,128)(2,1)} %text.5), channel_id=1, source_target_pairs={{1,3},{3,5},{5,7},{7,9},{9,11},{11,13},{13,15},{15,17},{17,19},{19... | collective-permute-start | bytes 2359304 | tf_op jit(solution)/shard_map/ppermute | solution.py:22
  9.1 0.7 collective-permute-start.3
  9.8 0.0 copy-start
  9.8 1.1 %copy-done = bf16[512,768]{1,0:T(8,128)(2,1)S(1)} copy-done((bf16[512,768]{1,0:T(8,128)(2,1)S(1)}, bf16[512,768]{1,0:T(8,128)(2,1)}, u32[]{:S(2)}) %copy-start) | copy-done | bytes 786456
  10.9 0.0 copy-start.2
  10.9 1.1 %copy-done.2 = bf16[512,768]{1,0:T(8,128)(2,1)S(1)} copy-done((bf16[512,768]{1,0:T(8,128)(2,1)S(1)}, bf16[512,768]{1,0:T(8,128)(2,1)}, u32[]{:S(2)}) %copy-start.2) | copy-done | bytes 786456
  12.1 0.7 prepare.1
  12.8 0.1 fusion.1
  12.9 14.7 %collective-permute-start = (bf16[256,768]{1,0:T(8,128)(2,1)S(1)}, bf16[256,768]{1,0:T(8,128)(2,1)S(1)}, u32[]{:S(2)}, u32[]{:S(2)}) collective-permute-start(bf16[256,768]{1,0:T(8,128)(2,1)S(1)} %get-tuple-element.40), channel_id=1, source_target_pairs={{0,1},{1,0},{2,3},{3,2},{4,5},{5,4},{6,7},{7,6},{8,9},{9,8},{10,11... | collective-permute-start | bytes 1179656 | tf_op jit(solution)/shard_map/ppermute | solution.py:22
  27.5 1.9 %collective-permute-start.1 = (bf16[256,768]{1,0:T(8,128)(2,1)S(1)}, bf16[256,768]{1,0:T(8,128)(2,1)S(1)}, u32[]{:S(2)}, u32[]{:S(2)}) collective-permute-start(bf16[256,768]{1,0:T(8,128)(2,1)S(1)} %get-tuple-element.39), channel_id=1, source_target_pairs={{0,1},{1,0},{2,3},{3,2},{4,5},{5,4},{6,7},{7,6},{8,9},{9,8},{10,11... | collective-permute-start | bytes 1179656 | tf_op jit(solution)/shard_map/ppermute | solution.py:22
  30.8 0.0 collective-permute-done.refs_0_
  30.8 0.4 collective-permute-done.1.refs_1_
  31.2 3.9 %local.1 = (f32[512,768]{1,0:T(8,128)S(1)}, f32[512,768]{1,0:T(8,128)S(1)}, f32[512,1]{1,0:T(8,128)S(1)}, f32[512,1]{1,0:T(8,128)S(1)}, bf16[512,768]{1,0:T(8,128)(2,1)S(1)}) custom-call(f32[1]{0:T(128)S(6)} %copy.11.scale, f32[1]{0:T(128)S(6)} %copy.12.shift, bf16[512,768]{1,0:T(8,128)(2,1)S(1)} %get-tuple-element.22.xlow, ...), custom_call_target="tpu_custom_call" | custom-call | flops 1 | bytes 1 | tf_op jit(solution)/shard_map/local/pallas_call | solution.py:204
  35.1 0.0 copy-start.1
  35.1 0.0 copy-start.3
  35.1 2.3 %collective-permute-start.6 = (bf16[512,768]{1,0:T(8,128)(2,1)S(1)}, bf16[512,768]{1,0:T(8,128)(2,1)S(1)}, u32[]{:S(2)}, u32[]{:S(2)}) collective-permute-start(bf16[512,768]{1,0:T(8,128)(2,1)S(1)} %get-tuple-element.31), channel_id=1, source_target_pairs={{0,2},{1,767},{2,4},{3,1},{4,6},{5,3},{6,8},{7,5},{8,10},{9,7},{10... | collective-permute-start | bytes 2359304 | tf_op jit(solution)/shard_map/ppermute | solution.py:22
  37.4 10.5 %collective-permute-done.2.text_piece = bf16[512,768]{1,0:T(8,128)(2,1)S(1)} collective-permute-done((bf16[512,768]{1,0:T(8,128)(2,1)}, bf16[512,768]{1,0:T(8,128)(2,1)S(1)}, u32[]{:S(2)}, u32[]{:S(2)}) %collective-permute-start.2) | collective-permute-done | bytes 786464 | tf_op jit(solution)/shard_map/ppermute | solution.py:22
  47.9 0.0 collective-permute-done.3.image_piece
  47.9 0.4 arrived.1.low
  48.3 0.1 fusion
  48.3 14.9 %collective-permute-start.4 = (bf16[256,768]{1,0:T(8,128)(2,1)S(1)}, bf16[256,768]{1,0:T(8,128)(2,1)S(1)}, u32[]{:S(2)}, u32[]{:S(2)}) collective-permute-start(bf16[256,768]{1,0:T(8,128)(2,1)S(1)} %get-tuple-element.38), channel_id=1, source_target_pairs={{0,1},{1,0},{2,3},{3,2},{4,5},{5,4},{6,7},{7,6},{8,9},{9,8},{10,11... | collective-permute-start | bytes 1179656 | tf_op jit(solution)/shard_map/ppermute | solution.py:22
  63.2 1.9 %collective-permute-start.5 = (bf16[256,768]{1,0:T(8,128)(2,1)S(1)}, bf16[256,768]{1,0:T(8,128)(2,1)S(1)}, u32[]{:S(2)}, u32[]{:S(2)}) collective-permute-start(bf16[256,768]{1,0:T(8,128)(2,1)S(1)} %get-tuple-element.37), channel_id=1, source_target_pairs={{0,1},{1,0},{2,3},{3,2},{4,5},{5,4},{6,7},{7,6},{8,9},{9,8},{10,11... | collective-permute-start | bytes 1179656 | tf_op jit(solution)/shard_map/ppermute | solution.py:22
  65.1 0.0 copy-done.1
  65.1 0.0 copy-done.3
  65.2 2.6 %first.1 = (f32[512,768]{1,0:T(8,128)}, f32[512,768]{1,0:T(8,128)}, f32[512,1]{1,0:T(8,128)S(1)}) custom-call(f32[1]{0:T(128)S(6)} %copy.11.scale, f32[1]{0:T(128)S(6)} %copy.12.shift, bf16[512,768]{1,0:T(8,128)(2,1)S(1)} %copy-done.1, bf16[512,768]{1,0:T(8,128)(2,1)S(1)} %copy-done.3, bf16[512,768]{1,0:T(8,128)(2,1)S(1)} %get-tuple-element.22.xlow, ...), custom_call_target="tpu_custom_call" | custom-call | flops 1 | bytes 1 | tf_op jit(solution)/shard_map/first/pallas_call | solution.py:204
  67.8 0.0 collective-permute-done.4.refs_0_
  67.8 0.0 collective-permute-done.5.refs_1_
  67.8 1.8 %second.1 = (f32[512,768]{1,0:T(8,128)S(1)}, f32[512,1]{1,0:T(8,128)S(1)}) custom-call(f32[1]{0:T(128)S(6)} %copy.11.scale, f32[1]{0:T(128)S(6)} %copy.12.shift, bf16[512,768]{1,0:T(8,128)(2,1)S(1)} %get-tuple-element.20.ylow, f32[512,768]{1,0:T(8,128)S(1)} %get-tuple-element.23.yacc_in, f32[512,1]{1,0:T(8,128)S(1)} %get-tuple-element.24.yloss_in, ...), custom_call_target="tpu_custom_call" | custom-call | flops 1 | bytes 1 | tf_op jit(solution)/shard_map/second/pallas_call | solution.py:204
  69.7 4.3 %collective-permute-done.6.low = bf16[512,768]{1,0:T(8,128)(2,1)S(1)} collective-permute-done((bf16[512,768]{1,0:T(8,128)(2,1)S(1)}, bf16[512,768]{1,0:T(8,128)(2,1)S(1)}, u32[]{:S(2)}, u32[]{:S(2)}) %collective-permute-start.6) | collective-permute-done | bytes 786464 | tf_op jit(solution)/shard_map/ppermute | solution.py:22
  74.0 3.2 %last.1 = (f32[512,768]{1,0:T(8,128)}, f32[512,768]{1,0:T(8,128)}, f32[512]{0:T(512)}) custom-call(f32[1]{0:T(128)S(6)} %copy.11.scale, f32[1]{0:T(128)S(6)} %copy.12.shift, bf16[512,768]{1,0:T(8,128)(2,1)S(1)} %copy-done.1, bf16[512,768]{1,0:T(8,128)(2,1)S(1)} %copy-done.3, ...), custom_call_target="tpu_custom_call", output_to_operand_aliasing={{0}: (9, {}), {1}: (10, {})} | custom-call | flops 1 | bytes 1 | tf_op jit(solution)/shard_map/last/pallas_call | solution.py:204
Async XLA Ops:
  0.6 47.3 %collective-permute-start.2 = (bf16[512,768]{1,0:T(8,128)(2,1)}, bf16[512,768]{1,0:T(8,128)(2,1)S(1)}, u32[]{:S(2)}, u32[]{:S(2)}) collective-permute-start(bf16[512,768]{1,0:T(8,128)(2,1)} %text.5), channel_id=1, source_target_pairs={{1,3},{3,5},{5,7},{7,9},{9,11},{11,13},{13,15},{15,17},{17,19},{19... | collective-permute-start | bytes 2359304 | tf_op jit(solution)/shard_map/ppermute | solution.py:22
  9.1 38.8 %collective-permute-start.3 = (bf16[512,768]{1,0:T(8,128)(2,1)}, bf16[512,768]{1,0:T(8,128)(2,1)S(1)}, u32[]{:S(2)}, u32[]{:S(2)}) collective-permute-start(bf16[512,768]{1,0:T(8,128)(2,1)} %image.5), channel_id=1, source_target_pairs={{0,766},{2,0},{4,2},{6,4},{8,6},{10,8},{12,10},{14,12},{16,14},{18... | collective-permute-start | bytes 2359304 | tf_op jit(solution)/shard_map/ppermute | solution.py:22
  9.8 1.1 %copy-start = (bf16[512,768]{1,0:T(8,128)(2,1)S(1)}, bf16[512,768]{1,0:T(8,128)(2,1)}, u32[]{:S(2)}) copy-start(bf16[512,768]{1,0:T(8,128)(2,1)} %image.5) | copy-start | bytes 2359300
  10.9 1.1 %copy-start.2 = (bf16[512,768]{1,0:T(8,128)(2,1)S(1)}, bf16[512,768]{1,0:T(8,128)(2,1)}, u32[]{:S(2)}) copy-start(bf16[512,768]{1,0:T(8,128)(2,1)} %text.5) | copy-start | bytes 2359300
  12.9 17.9 %collective-permute-start = (bf16[256,768]{1,0:T(8,128)(2,1)S(1)}, bf16[256,768]{1,0:T(8,128)(2,1)S(1)}, u32[]{:S(2)}, u32[]{:S(2)}) collective-permute-start(bf16[256,768]{1,0:T(8,128)(2,1)S(1)} %get-tuple-element.40), channel_id=1, source_target_pairs={{0,1},{1,0},{2,3},{3,2},{4,5},{5,4},{6,7},{7,6},{8,9},{9,8},{10,11... | collective-permute-start | bytes 1179656 | tf_op jit(solution)/shard_map/ppermute | solution.py:22
  27.5 3.6 %collective-permute-start.1 = (bf16[256,768]{1,0:T(8,128)(2,1)S(1)}, bf16[256,768]{1,0:T(8,128)(2,1)S(1)}, u32[]{:S(2)}, u32[]{:S(2)}) collective-permute-start(bf16[256,768]{1,0:T(8,128)(2,1)S(1)} %get-tuple-element.39), channel_id=1, source_target_pairs={{0,1},{1,0},{2,3},{3,2},{4,5},{5,4},{6,7},{7,6},{8,9},{9,8},{10,11... | collective-permute-start | bytes 1179656 | tf_op jit(solution)/shard_map/ppermute | solution.py:22
  35.1 30.1 %copy-start.1 = (bf16[512,768]{1,0:T(8,128)(2,1)S(1)}, bf16[512,768]{1,0:T(8,128)(2,1)}, u32[]{:S(2)}) copy-start(bf16[512,768]{1,0:T(8,128)(2,1)} %image.5) | copy-start | bytes 2359300
  35.1 30.0 %copy-start.3 = (bf16[512,768]{1,0:T(8,128)(2,1)S(1)}, bf16[512,768]{1,0:T(8,128)(2,1)}, u32[]{:S(2)}) copy-start(bf16[512,768]{1,0:T(8,128)(2,1)} %text.5) | copy-start | bytes 2359300
  35.1 38.9 %collective-permute-start.6 = (bf16[512,768]{1,0:T(8,128)(2,1)S(1)}, bf16[512,768]{1,0:T(8,128)(2,1)S(1)}, u32[]{:S(2)}, u32[]{:S(2)}) collective-permute-start(bf16[512,768]{1,0:T(8,128)(2,1)S(1)} %get-tuple-element.31), channel_id=1, source_target_pairs={{0,2},{1,767},{2,4},{3,1},{4,6},{5,3},{6,8},{7,5},{8,10},{9,7},{10... | collective-permute-start | bytes 2359304 | tf_op jit(solution)/shard_map/ppermute | solution.py:22
  48.3 19.5 %collective-permute-start.4 = (bf16[256,768]{1,0:T(8,128)(2,1)S(1)}, bf16[256,768]{1,0:T(8,128)(2,1)S(1)}, u32[]{:S(2)}, u32[]{:S(2)}) collective-permute-start(bf16[256,768]{1,0:T(8,128)(2,1)S(1)} %get-tuple-element.38), channel_id=1, source_target_pairs={{0,1},{1,0},{2,3},{3,2},{4,5},{5,4},{6,7},{7,6},{8,9},{9,8},{10,11... | collective-permute-start | bytes 1179656 | tf_op jit(solution)/shard_map/ppermute | solution.py:22
  63.2 4.6 %collective-permute-start.5 = (bf16[256,768]{1,0:T(8,128)(2,1)S(1)}, bf16[256,768]{1,0:T(8,128)(2,1)S(1)}, u32[]{:S(2)}, u32[]{:S(2)}) collective-permute-start(bf16[256,768]{1,0:T(8,128)(2,1)S(1)} %get-tuple-element.37), channel_id=1, source_target_pairs={{0,1},{1,0},{2,3},{3,2},{4,5},{5,4},{6,7},{7,6},{8,9},{9,8},{10,11... | collective-permute-start | bytes 1179656 | tf_op jit(solution)/shard_map/ppermute | solution.py:22

commit v2 on v1

--- a/solution.py
+++ b/solution.py
@@ -11,7 +11,6 @@
 F32 = jnp.float32
 BF16 = jnp.bfloat16
 VMEM = pl.BlockSpec(memory_space=pltpu.VMEM)
-SMEM = pl.BlockSpec(memory_space=pltpu.SMEM)
 ANY = pl.BlockSpec(memory_space=pl.ANY)
 PARAMS = pltpu.CompilerParams(vmem_limit_bytes=16 * 2**20)
 
@@ -77,18 +76,6 @@
     return (grad - unit * jnp.sum(unit * grad, axis=-1, keepdims=True)) * inverse
 
 
-def put(grad, odd, image_grad, text_grad, sems, number, act):
-    at = pl.ds(number * TILE, TILE)
-
-    @pl.when(odd)
-    def _():
-        act(pltpu.make_async_copy(grad.at[at, :], image_grad.at[at, :], sems.at[number]))
-
-    @pl.when(jnp.logical_not(odd))
-    def _():
-        act(pltpu.make_async_copy(grad.at[at, :], text_grad.at[at, :], sems.at[number]))
-
-
 def prepare_kernel(image, text, xlow, ylow, xinv, yinv):
     odd = is_odd()
     for start in range(0, image.shape[0], TILE):
@@ -112,7 +99,7 @@
 
 def local_kernel(scale, shift, xlow, ylow, *refs):
     pieces, (xacc, yacc, xloss, yloss, xsend) = refs[:-5], refs[-5:]
-    temper, offset = scale[0], shift[0]
+    temper, offset = scale[...], shift[...]
     rows = xlow.shape[0]
     for start in range(0, rows, TILE):
         at = pl.ds(start, TILE)
@@ -131,57 +118,88 @@
         yacc[at, :] = weighted(coef, xlow[...])
 
 
-def first_kernel(
-    scale, shift, image, text, xlow, xinv, xacc, xloss_in, low,
-    image_grad, text_grad, xloss, grad, sems,
-):
-    temper, offset = scale[0], shift[0]
-    odd = is_odd()
-    count = xlow.shape[0] // TILE
-    for number in range(count):
-        at = pl.ds(number * TILE, TILE)
-        coef, plus = terms(products(xlow[at, :], low[...], temper, offset))
+def first_kernel(scale, shift, image, text, xlow, xinv, xacc, xloss_in, low, grad, xloss):
+    temper, offset = scale[...], shift[...]
+    odd = is_odd()
+    starts = range(0, xlow.shape[0], TILE)
+    logits = [products(xlow[pl.ds(start, TILE), :], low[...], temper, offset) for start in starts]
+    for start, tile in zip(starts, logits):
+        at = pl.ds(start, TILE)
+        coef, plus = terms(tile)
         xloss[at, :] = xloss_in[at, :] + plus
         acc = xacc[at, :] + weighted(coef, low[...])
         grad[at, :] = finished(acc, select(odd, image, text, at), xinv[at, :], temper)
-        put(grad, odd, image_grad, text_grad, sems, number, lambda copy: copy.start())
-    for number in range(count):
-        put(grad, odd, image_grad, text_grad, sems, number, lambda copy: copy.wait())
-
-
-def second_kernel(scale, shift, ylow, yacc_in, yloss_in, xloss, *refs):
-    pieces, (yacc, loss) = refs[:-2], refs[-2:]
-    temper, offset = scale[0], shift[0]
-    odd = is_odd()
-    for start in range(0, ylow.shape[0], TILE):
-        at = pl.ds(start, TILE)
-        total, acc = yloss_in[at, :], yacc_in[at, :]
-        for piece in pieces:
-            coef, plus = terms(products(ylow[at, :], piece[...], temper, offset))
-            total += plus
-            acc += weighted(coef, piece[...])
-        loss[at, :] = jnp.where(odd, xloss[at, :], total)
-        yacc[at, :] = acc
+
+
+def second_kernel(scale, shift, ylow, yacc_in, yloss_in, xloss, xgrad, *refs):
+    pieces, (yacc, loss, image_grad, text_grad, sem) = refs[:-5], refs[-5:]
+    temper, offset = scale[...], shift[...]
+    odd = is_odd()
+
+    def run(target):
+        copy = pltpu.make_async_copy(xgrad, target, sem)
+        copy.start()
+        starts = range(0, ylow.shape[0], TILE)
+        logits = [
+            [products(ylow[pl.ds(start, TILE), :], piece[...], temper, offset) for piece in pieces]
+            for start in starts
+        ]
+        for start, tiles in zip(starts, logits):
+            at = pl.ds(start, TILE)
+            total, acc = yloss_in[at, :], yacc_in[at, :]
+            for piece, tile in zip(pieces, tiles):
+                coef, plus = terms(tile)
+                total += plus
+                acc += weighted(coef, piece[...])
+            loss[at, :] = jnp.where(odd, xloss[at, :], total)
+            yacc[at, :] = acc
+        copy.wait()
+
+    @pl.when(odd)
+    def _():
+        run(image_grad)
+
+    @pl.when(jnp.logical_not(odd))
+    def _():
+        run(text_grad)
 
 
 def last_kernel(
     scale, shift, image, text, ylow, yinv, yacc, loss_in, low, image_in, text_in,
-    image_grad, text_grad, loss, grad, sems,
+    image_grad, text_grad, loss, ygrad, sems,
 ):
     del image_in, text_in
-    temper, offset = scale[0], shift[0]
-    odd = is_odd()
-    rows = ylow.shape[0]
-    for number in range(rows // TILE):
-        at = pl.ds(number * TILE, TILE)
-        coef, plus = terms(products(ylow[at, :], low[...], temper, offset))
-        acc = yacc[at, :] + weighted(coef, low[...])
-        grad[at, :] = finished(acc, select(odd, text, image, at), yinv[at, :], temper)
-        put(grad, jnp.logical_not(odd), image_grad, text_grad, sems, number, lambda copy: copy.start())
-        total = loss_in[at, :] + jnp.where(odd, 0.0, plus)
-        loss[at] = jnp.sum(total, axis=1) * (1.0 / rows)
-    for number in range(rows // TILE):
-        put(grad, jnp.logical_not(odd), image_grad, text_grad, sems, number, lambda copy: copy.wait())
+    temper, offset = scale[...], shift[...]
+    odd = is_odd()
+
+    def run(raw, target, counted):
+        rows = ylow.shape[0]
+        starts = range(0, rows, TILE)
+        copies = [
+            pltpu.make_async_copy(
+                ygrad.at[pl.ds(start, TILE), :], target.at[pl.ds(start, TILE), :], sems.at[start // TILE]
+            )
+            for start in starts
+        ]
+        logits = [products(ylow[pl.ds(start, TILE), :], low[...], temper, offset) for start in starts]
+        for start, tile, copy in zip(starts, logits, copies):
+            at = pl.ds(start, TILE)
+            coef, plus = terms(tile)
+            acc = yacc[at, :] + weighted(coef, low[...])
+            ygrad[at, :] = finished(acc, raw[at, :].astype(F32), yinv[at, :], temper)
+            copy.start()
+            total = loss_in[at, :] + plus if counted else loss_in[at, :]
+            loss[at] = jnp.sum(total, axis=1) * (1.0 / rows)
+        for copy in copies:
+            copy.wait()
+
+    @pl.when(odd)
+    def _():
+        run(text, text_grad, False)
+
+    @pl.when(jnp.logical_not(odd))
+    def _():
+        run(image, image_grad, True)
 
 
 def cost():
@@ -196,7 +214,6 @@
     wide = jax.ShapeDtypeStruct((rows, width), F32)
     slim = jax.ShapeDtypeStruct((rows, width), BF16)
     thin = jax.ShapeDtypeStruct((rows, 1), F32)
-    grads = [pltpu.VMEM((rows, width), F32), pltpu.SemaphoreType.DMA((rows // TILE,))]
 
     def call(kernel, name, inputs, outs, **more):
         specs = dict(out_specs=(VMEM,) * len(outs), in_specs=[VMEM] * len(inputs))
@@ -205,30 +222,28 @@
             kernel, out_shape=outs, compiler_params=PARAMS, cost_estimate=cost(), name=name, **specs
         )(*inputs)
 
-    numbers = (scale, shift)
+    numbers = (scale.reshape(1, 1), shift.reshape(1, 1))
     xlow, ylow, xinv, yinv = call(prepare_kernel, "prepare", (image, text), (slim, slim, thin, thin))
     r0 = exchange_in_parts(xlow, 2, -1, 1)
     xacc, yacc, xloss, yloss, xsend = call(
         local_kernel, "local", (*numbers, xlow, ylow, *r0), (wide, wide, thin, thin, slim),
-        in_specs=[SMEM] * 2 + [VMEM] * (2 + len(r0)),
     )
     r2 = exchange(xsend, -2, 2)
     (r1,) = call(arrived_kernel, "arrived", (text_piece, image_piece), (slim,))
     r3 = exchange_in_parts(r1, 2, -1, 1)
-    image_grad, text_grad, xloss = call(
-        first_kernel, "first", (*numbers, image, text, xlow, xinv, xacc, xloss, r1), (wide, wide, thin),
-        in_specs=[SMEM] * 2 + [VMEM] * 7, out_specs=(ANY, ANY, VMEM), scratch_shapes=grads,
-    )
-    yacc, loss = call(
-        second_kernel, "second", (*numbers, ylow, yacc, yloss, xloss, *r3), (wide, thin),
-        in_specs=[SMEM] * 2 + [VMEM] * (4 + len(r3)),
+    xgrad, xloss = call(
+        first_kernel, "first", (*numbers, image, text, xlow, xinv, xacc, xloss, r1), (wide, thin)
+    )
+    yacc, loss, image_grad, text_grad = call(
+        second_kernel, "second", (*numbers, ylow, yacc, yloss, xloss, xgrad, *r3), (wide, thin, wide, wide),
+        out_specs=(VMEM, VMEM, ANY, ANY), scratch_shapes=[pltpu.SemaphoreType.DMA],
     )
     image_grad, text_grad, loss = call(
         last_kernel, "last",
         (*numbers, image, text, ylow, yinv, yacc, loss, r2, image_grad, text_grad),
         (wide, wide, jax.ShapeDtypeStruct((rows,), F32)),
-        in_specs=[SMEM] * 2 + [VMEM] * 7 + [ANY] * 2, out_specs=(ANY, ANY, VMEM), scratch_shapes=grads,
-        input_output_aliases={9: 0, 10: 1},
+        in_specs=[VMEM] * 9 + [ANY] * 2, out_specs=(ANY, ANY, VMEM), input_output_aliases={9: 0, 10: 1},
+        scratch_shapes=[pltpu.VMEM((rows, width), F32), pltpu.SemaphoreType.DMA((rows // TILE,))],
     )
     return loss, image_grad, text_grad
 

time: 77.6 us -> 76.5 us (0.986)
  waiting for transfers between devices: 15.2 us -> 23 us
  starting transfers between devices: 44.8 us -> 38.1 us
  Pallas kernels: 12.7 us -> 10.6 us
    ppermute x7, waiting for transfers between devices: 15.2 us -> 23 us  [exchange(): lax.ppermute(array, AXES, [(i, (i + by) % count) for i, by in steps if by...]
    ppermute x7, starting transfers between devices: 44.8 us -> 38.1 us  [exchange(): lax.ppermute(array, AXES, [(i, (i + by) % count) for i, by in steps if by...]
    pallas_call x6, Pallas kernels: 12.7 us -> 10.6 us  [call(): pl.pallas_call(kernel, out_shape=outs, compiler_params=PARAMS, cost_estim...]
  transfers between devices with their start and end apart: 7 -> 7, of which waited for: 3 -> 3; matrix products, arithmetic and copies ran while one was open for 0% -> 0% of each run, Pallas kernels for 12% -> 10%
where the time goes in v2:
time: 76.5 us; the launch traced here: 76.1 us
  starting transfers between devices  38.1 us (50%)
  waiting for transfers between devices  23 us (30%)
  Pallas kernels  10.6 us (14%)
  local copies, waits for them, and re-layouts  2.38 us (3%)
  between operations  2.09 us (3%)
    ppermute x7, starting transfers between devices, exchange(): lax.ppermute(array, AXES, [(i, (i + by) % count) for i, by in steps if by...  38.1 us
    ppermute x7, waiting for transfers between devices, exchange(): lax.ppermute(array, AXES, [(i, (i + by) % count) for i, by in steps if by...  23 us
    pallas_call x6, Pallas kernels, call(): pl.pallas_call(kernel, out_shape=outs, compiler_params=PARAMS, cost_estim...  10.6 us
    unnamed x8, local copies, waits for them, and re-layouts  2.27 us
  transfers between devices with their start and end apart: 7, of which 3 were waited for; matrix products, arithmetic and copies ran while one was open for 0% of the time, Pallas kernels for 10%

profile of v2, /device:TPU:1, one launch (start us, length us, event | category | flops | bytes accessed | tf_op | source)
XLA Modules:
  0.0 76.1 jit_solution(3489444338720964685)
XLA Ops:
  0.6 0.7 collective-permute-start.3
  1.3 8.4 %collective-permute-start.2 = (bf16[512,768]{1,0:T(8,128)(2,1)}, bf16[512,768]{1,0:T(8,128)(2,1)S(1)}, u32[]{:S(2)}, u32[]{:S(2)}) collective-permute-start(bf16[512,768]{1,0:T(8,128)(2,1)} %text.5), channel_id=1, source_target_pairs={{1,3},{3,5},{5,7},{7,9},{9,11},{11,13},{13,15},{15,17},{17,19},{19... | collective-permute-start | bytes 2359304 | tf_op jit(solution)/shard_map/ppermute | solution.py:21
  9.8 0.0 copy-start
  9.8 1.1 %copy-done = bf16[512,768]{1,0:T(8,128)(2,1)S(1)} copy-done((bf16[512,768]{1,0:T(8,128)(2,1)S(1)}, bf16[512,768]{1,0:T(8,128)(2,1)}, u32[]{:S(2)}) %copy-start) | copy-done | bytes 786456
  10.9 0.0 copy-start.2
  10.9 1.1 %copy-done.2 = bf16[512,768]{1,0:T(8,128)(2,1)S(1)} copy-done((bf16[512,768]{1,0:T(8,128)(2,1)S(1)}, bf16[512,768]{1,0:T(8,128)(2,1)}, u32[]{:S(2)}) %copy-start.2) | copy-done | bytes 786456
  12.1 0.7 prepare.1
  12.8 0.1 fusion.1
  12.9 14.7 %collective-permute-start.1 = (bf16[256,768]{1,0:T(8,128)(2,1)S(1)}, bf16[256,768]{1,0:T(8,128)(2,1)S(1)}, u32[]{:S(2)}, u32[]{:S(2)}) collective-permute-start(bf16[256,768]{1,0:T(8,128)(2,1)S(1)} %get-tuple-element.41), channel_id=1, source_target_pairs={{0,1},{1,0},{2,3},{3,2},{4,5},{5,4},{6,7},{7,6},{8,9},{9,8},{10,11... | collective-permute-start | bytes 1179656 | tf_op jit(solution)/shard_map/ppermute | solution.py:21
  27.5 1.9 %collective-permute-start = (bf16[256,768]{1,0:T(8,128)(2,1)S(1)}, bf16[256,768]{1,0:T(8,128)(2,1)S(1)}, u32[]{:S(2)}, u32[]{:S(2)}) collective-permute-start(bf16[256,768]{1,0:T(8,128)(2,1)S(1)} %get-tuple-element.42), channel_id=1, source_target_pairs={{0,1},{1,0},{2,3},{3,2},{4,5},{5,4},{6,7},{7,6},{8,9},{9,8},{10,11... | collective-permute-start | bytes 1179656 | tf_op jit(solution)/shard_map/ppermute | solution.py:21
  30.7 0.0 collective-permute-done.1.refs_1_
  30.8 0.4 collective-permute-done.refs_0_
  31.1 3.9 %local.1 = (f32[512,768]{1,0:T(8,128)S(1)}, f32[512,768]{1,0:T(8,128)S(1)}, f32[512,1]{1,0:T(8,128)S(1)}, f32[512,1]{1,0:T(8,128)S(1)}, bf16[512,768]{1,0:T(8,128)(2,1)S(1)}) custom-call(f32[1,1]{1,0:T(1,128)} %bitcast.2.scale, f32[1,1]{1,0:T(1,128)} %bitcast.6.shift, bf16[512,768]{1,0:T(8,128)(2,1)S(1)} %get-tuple-element.23.xlow, ...), custom_call_target="tpu_custom_call" | custom-call | flops 1 | bytes 1 | tf_op jit(solution)/shard_map/local/pallas_call | solution.py:221
  35.0 0.0 copy-start.1
  35.0 0.0 copy-start.3
  35.1 2.3 %collective-permute-start.6 = (bf16[512,768]{1,0:T(8,128)(2,1)S(1)}, bf16[512,768]{1,0:T(8,128)(2,1)S(1)}, u32[]{:S(2)}, u32[]{:S(2)}) collective-permute-start(bf16[512,768]{1,0:T(8,128)(2,1)S(1)} %get-tuple-element.33), channel_id=1, source_target_pairs={{0,2},{1,767},{2,4},{3,1},{4,6},{5,3},{6,8},{7,5},{8,10},{9,7},{10... | collective-permute-start | bytes 2359304 | tf_op jit(solution)/shard_map/ppermute | solution.py:21
  37.4 0.0 collective-permute-done.3.image_piece
  37.4 13.1 %collective-permute-done.2.text_piece = bf16[512,768]{1,0:T(8,128)(2,1)S(1)} collective-permute-done((bf16[512,768]{1,0:T(8,128)(2,1)}, bf16[512,768]{1,0:T(8,128)(2,1)S(1)}, u32[]{:S(2)}, u32[]{:S(2)}) %collective-permute-start.2) | collective-permute-done | bytes 786464 | tf_op jit(solution)/shard_map/ppermute | solution.py:21
  50.5 0.4 arrived.1.low
  50.8 0.1 fusion
  50.9 8.1 %collective-permute-start.5 = (bf16[256,768]{1,0:T(8,128)(2,1)S(1)}, bf16[256,768]{1,0:T(8,128)(2,1)S(1)}, u32[]{:S(2)}, u32[]{:S(2)}) collective-permute-start(bf16[256,768]{1,0:T(8,128)(2,1)S(1)} %get-tuple-element.39), channel_id=1, source_target_pairs={{0,1},{1,0},{2,3},{3,2},{4,5},{5,4},{6,7},{7,6},{8,9},{9,8},{10,11... | collective-permute-start | bytes 1179656 | tf_op jit(solution)/shard_map/ppermute | solution.py:21
  59.0 1.9 %collective-permute-start.4 = (bf16[256,768]{1,0:T(8,128)(2,1)S(1)}, bf16[256,768]{1,0:T(8,128)(2,1)S(1)}, u32[]{:S(2)}, u32[]{:S(2)}) collective-permute-start(bf16[256,768]{1,0:T(8,128)(2,1)S(1)} %get-tuple-element.40), channel_id=1, source_target_pairs={{0,1},{1,0},{2,3},{3,2},{4,5},{5,4},{6,7},{7,6},{8,9},{9,8},{10,11... | collective-permute-start | bytes 1179656 | tf_op jit(solution)/shard_map/ppermute | solution.py:21
  61.0 0.0 copy-done.1
  61.0 0.0 copy-done.3
  61.0 1.6 %first.1 = (f32[512,768]{1,0:T(8,128)S(1)}, f32[512,1]{1,0:T(8,128)S(1)}) custom-call(f32[1,1]{1,0:T(1,128)} %bitcast.3.scale, f32[1,1]{1,0:T(1,128)} %bitcast.7.shift, bf16[512,768]{1,0:T(8,128)(2,1)S(1)} %copy-done.1, bf16[512,768]{1,0:T(8,128)(2,1)S(1)} %copy-done.3, bf16[512,768]{1,0:T(8,128)(2,1)S(1)} %get-tuple-element.23.xlow, ...), custom_call_target="tpu_custom_call" | custom-call | flops 1 | bytes 1 | tf_op jit(solution)/shard_map/first/pallas_call | solution.py:221
  62.6 0.0 collective-permute-done.5.refs_1_
  62.6 0.0 collective-permute-done.4.refs_0_
  62.7 1.2 %second.1 = (f32[512,768]{1,0:T(8,128)S(1)}, f32[512,1]{1,0:T(8,128)S(1)}, f32[512,768]{1,0:T(8,128)}, f32[512,768]{1,0:T(8,128)}) custom-call(f32[1,1]{1,0:T(1,128)} %bitcast.4.scale, f32[1,1]{1,0:T(1,128)} %bitcast.8.shift, bf16[512,768]{1,0:T(8,128)(2,1)S(1)} %get-tuple-element.21.ylow, f32[512,768]{1,0:T(8,128)S(1)} %get-tuple-element.24.yacc_in, ...), custom_call_target="tpu_custom_call" | custom-call | flops 1 | bytes 1 | tf_op jit(solution)/shard_map/second/pallas_call | solution.py:221
  63.8 9.4 %collective-permute-done.6.low = bf16[512,768]{1,0:T(8,128)(2,1)S(1)} collective-permute-done((bf16[512,768]{1,0:T(8,128)(2,1)S(1)}, bf16[512,768]{1,0:T(8,128)(2,1)S(1)}, u32[]{:S(2)}, u32[]{:S(2)}) %collective-permute-start.6) | collective-permute-done | bytes 786464 | tf_op jit(solution)/shard_map/ppermute | solution.py:21
  73.3 2.8 %last.1 = (f32[512,768]{1,0:T(8,128)}, f32[512,768]{1,0:T(8,128)}, f32[512]{0:T(512)}) custom-call(f32[1,1]{1,0:T(1,128)} %bitcast.5.scale, f32[1,1]{1,0:T(1,128)} %bitcast.9.shift, bf16[512,768]{1,0:T(8,128)(2,1)S(1)} %copy-done.1, bf16[512,768]{1,0:T(8,128)(2,1)S(1)} %copy-done.3, ...), custom_call_target="tpu_custom_call", output_to_operand_aliasing={{0}: (9, {}), {1}: (10, {})} | custom-call | flops 1 | bytes 1 | tf_op jit(solution)/shard_map/last/pallas_call | solution.py:221
Async XLA Ops:
  0.6 36.7 %collective-permute-start.3 = (bf16[512,768]{1,0:T(8,128)(2,1)}, bf16[512,768]{1,0:T(8,128)(2,1)S(1)}, u32[]{:S(2)}, u32[]{:S(2)}) collective-permute-start(bf16[512,768]{1,0:T(8,128)(2,1)} %image.5), channel_id=1, source_target_pairs={{0,766},{2,0},{4,2},{6,4},{8,6},{10,8},{12,10},{14,12},{16,14},{18... | collective-permute-start | bytes 2359304 | tf_op jit(solution)/shard_map/ppermute | solution.py:21
  1.3 49.1 %collective-permute-start.2 = (bf16[512,768]{1,0:T(8,128)(2,1)}, bf16[512,768]{1,0:T(8,128)(2,1)S(1)}, u32[]{:S(2)}, u32[]{:S(2)}) collective-permute-start(bf16[512,768]{1,0:T(8,128)(2,1)} %text.5), channel_id=1, source_target_pairs={{1,3},{3,5},{5,7},{7,9},{9,11},{11,13},{13,15},{15,17},{17,19},{19... | collective-permute-start | bytes 2359304 | tf_op jit(solution)/shard_map/ppermute | solution.py:21
  9.8 1.1 %copy-start = (bf16[512,768]{1,0:T(8,128)(2,1)S(1)}, bf16[512,768]{1,0:T(8,128)(2,1)}, u32[]{:S(2)}) copy-start(bf16[512,768]{1,0:T(8,128)(2,1)} %image.5) | copy-start | bytes 2359300
  10.9 1.1 %copy-start.2 = (bf16[512,768]{1,0:T(8,128)(2,1)S(1)}, bf16[512,768]{1,0:T(8,128)(2,1)}, u32[]{:S(2)}) copy-start(bf16[512,768]{1,0:T(8,128)(2,1)} %text.5) | copy-start | bytes 2359300
  12.9 17.9 %collective-permute-start.1 = (bf16[256,768]{1,0:T(8,128)(2,1)S(1)}, bf16[256,768]{1,0:T(8,128)(2,1)S(1)}, u32[]{:S(2)}, u32[]{:S(2)}) collective-permute-start(bf16[256,768]{1,0:T(8,128)(2,1)S(1)} %get-tuple-element.41), channel_id=1, source_target_pairs={{0,1},{1,0},{2,3},{3,2},{4,5},{5,4},{6,7},{7,6},{8,9},{9,8},{10,11... | collective-permute-start | bytes 1179656 | tf_op jit(solution)/shard_map/ppermute | solution.py:21
  27.5 3.6 %collective-permute-start = (bf16[256,768]{1,0:T(8,128)(2,1)S(1)}, bf16[256,768]{1,0:T(8,128)(2,1)S(1)}, u32[]{:S(2)}, u32[]{:S(2)}) collective-permute-start(bf16[256,768]{1,0:T(8,128)(2,1)S(1)} %get-tuple-element.42), channel_id=1, source_target_pairs={{0,1},{1,0},{2,3},{3,2},{4,5},{5,4},{6,7},{7,6},{8,9},{9,8},{10,11... | collective-permute-start | bytes 1179656 | tf_op jit(solution)/shard_map/ppermute | solution.py:21
  35.0 25.9 %copy-start.1 = (bf16[512,768]{1,0:T(8,128)(2,1)S(1)}, bf16[512,768]{1,0:T(8,128)(2,1)}, u32[]{:S(2)}) copy-start(bf16[512,768]{1,0:T(8,128)(2,1)} %image.5) | copy-start | bytes 2359300
  35.0 25.9 %copy-start.3 = (bf16[512,768]{1,0:T(8,128)(2,1)S(1)}, bf16[512,768]{1,0:T(8,128)(2,1)}, u32[]{:S(2)}) copy-start(bf16[512,768]{1,0:T(8,128)(2,1)} %text.5) | copy-start | bytes 2359300
  35.1 38.2 %collective-permute-start.6 = (bf16[512,768]{1,0:T(8,128)(2,1)S(1)}, bf16[512,768]{1,0:T(8,128)(2,1)S(1)}, u32[]{:S(2)}, u32[]{:S(2)}) collective-permute-start(bf16[512,768]{1,0:T(8,128)(2,1)S(1)} %get-tuple-element.33), channel_id=1, source_target_pairs={{0,2},{1,767},{2,4},{3,1},{4,6},{5,3},{6,8},{7,5},{8,10},{9,7},{10... | collective-permute-start | bytes 2359304 | tf_op jit(solution)/shard_map/ppermute | solution.py:21
  50.9 11.7 %collective-permute-start.5 = (bf16[256,768]{1,0:T(8,128)(2,1)S(1)}, bf16[256,768]{1,0:T(8,128)(2,1)S(1)}, u32[]{:S(2)}, u32[]{:S(2)}) collective-permute-start(bf16[256,768]{1,0:T(8,128)(2,1)S(1)} %get-tuple-element.39), channel_id=1, source_target_pairs={{0,1},{1,0},{2,3},{3,2},{4,5},{5,4},{6,7},{7,6},{8,9},{9,8},{10,11... | collective-permute-start | bytes 1179656 | tf_op jit(solution)/shard_map/ppermute | solution.py:21
  59.0 3.6 %collective-permute-start.4 = (bf16[256,768]{1,0:T(8,128)(2,1)S(1)}, bf16[256,768]{1,0:T(8,128)(2,1)S(1)}, u32[]{:S(2)}, u32[]{:S(2)}) collective-permute-start(bf16[256,768]{1,0:T(8,128)(2,1)S(1)} %get-tuple-element.40), channel_id=1, source_target_pairs={{0,1},{1,0},{2,3},{3,2},{4,5},{5,4},{6,7},{7,6},{8,9},{9,8},{10,11... | collective-permute-start | bytes 1179656 | tf_op jit(solution)/shard_map/ppermute | solution.py:21

commit v3 on v2

--- a/solution.py
+++ b/solution.py
@@ -15,10 +15,15 @@
 PARAMS = pltpu.CompilerParams(vmem_limit_bytes=16 * 2**20)
 
 
-def exchange(array, odd_by, even_by):
+def exchange(array, odd_by, even_by, among=None):
     count = lax.axis_size(AXES)
-    steps = [(i, odd_by if i % 2 else even_by) for i in range(count)]
+    steps = [(i, odd_by if i % 2 else even_by) for i in range(count) if among is None or among(i)]
     return lax.ppermute(array, AXES, [(i, (i + by) % count) for i, by in steps if by is not None])
+
+
+def crosses(index):
+    run = lax.axis_size("sub")
+    return index % run == 1 or index % run == run - 2
 
 
 def exchange_in_parts(array, parts, odd_by, even_by):
@@ -89,7 +94,8 @@
             low[at, :] = (full * inverse).astype(BF16)
 
 
-def arrived_kernel(text_piece, image_piece, low):
+def arrived_kernel(text_piece, image_piece, after, low):
+    del after
     odd = is_odd()
     for start in range(0, low.shape[0], TILE):
         at = pl.ds(start, TILE)
@@ -97,25 +103,37 @@
         low[at, :] = (full * inverse_norm(full)).astype(BF16)
 
 
-def local_kernel(scale, shift, xlow, ylow, *refs):
-    pieces, (xacc, yacc, xloss, yloss, xsend) = refs[:-5], refs[-5:]
+def local_kernel(scale, shift, xlow, ylow, acc, loss, xsend):
     temper, offset = scale[...], shift[...]
     rows = xlow.shape[0]
+    xsend[...] = xlow[...]
     for start in range(0, rows, TILE):
         at = pl.ds(start, TILE)
-        xsend[at, :] = xlow[at, :]
         diagonal = on_diagonal(start, TILE, rows)
         coef, plus = terms(products(xlow[at, :], ylow[...], temper, offset), diagonal)
-        acc = weighted(coef, ylow[...])
-        for piece in pieces:
-            coef, more = terms(products(xlow[at, :], piece[...], temper, offset))
-            plus += more
-            acc += weighted(coef, piece[...])
-        xloss[at, :] = plus
-        xacc[at, :] = acc
-        coef, plus = terms(products(ylow[at, :], xlow[...], temper, offset), diagonal)
+        loss[at, :] = plus
+        acc[at, :] = weighted(coef, ylow[...])
+
+
+def near_kernel(scale, shift, xlow, ylow, acc, loss, *refs):
+    pieces, (xacc, yacc, xloss, yloss, xsend) = refs[:-5], refs[-5:]
+    temper, offset = scale[...], shift[...]
+    rows = xlow.shape[0]
+    xsend[...] = xlow[...]
+    for start in range(0, rows, TILE):
+        at = pl.ds(start, TILE)
+        coef, plus = terms(
+            products(ylow[at, :], xlow[...], temper, offset), on_diagonal(start, TILE, rows)
+        )
         yloss[at, :] = plus
         yacc[at, :] = weighted(coef, xlow[...])
+        total, wide = loss[at, :], acc[at, :]
+        for piece in pieces:
+            coef, plus = terms(products(xlow[at, :], piece[...], temper, offset))
+            total += plus
+            wide += weighted(coef, piece[...])
+        xloss[at, :] = total
+        xacc[at, :] = wide
 
 
 def first_kernel(scale, shift, image, text, xlow, xinv, xacc, xloss_in, low, grad, xloss):
@@ -165,12 +183,16 @@
 
 
 def last_kernel(
-    scale, shift, image, text, ylow, yinv, yacc, loss_in, low, image_in, text_in,
-    image_grad, text_grad, loss, ygrad, sems,
+    scale, shift, image, text, ylow, yinv, yacc, loss_in, r2_across, r2, image_in, text_in,
+    image_grad, text_grad, loss, ygrad, sems, low,
 ):
     del image_in, text_in
     temper, offset = scale[...], shift[...]
     odd = is_odd()
+
+    place = lax.axis_index("sub")
+    across = jnp.logical_or(place == 0, place == lax.axis_size("sub") - 1)
+    low[...] = jnp.where(across, r2_across[...], r2[...])
 
     def run(raw, target, counted):
         rows = ylow.shape[0]
@@ -225,11 +247,15 @@
     numbers = (scale.reshape(1, 1), shift.reshape(1, 1))
     xlow, ylow, xinv, yinv = call(prepare_kernel, "prepare", (image, text), (slim, slim, thin, thin))
     r0 = exchange_in_parts(xlow, 2, -1, 1)
+    xacc, xloss, xsend = call(local_kernel, "local", (*numbers, xlow, ylow), (wide, thin, slim))
+    r2_across = exchange(xsend, -2, 2, crosses)
     xacc, yacc, xloss, yloss, xsend = call(
-        local_kernel, "local", (*numbers, xlow, ylow, *r0), (wide, wide, thin, thin, slim),
-    )
-    r2 = exchange(xsend, -2, 2)
-    (r1,) = call(arrived_kernel, "arrived", (text_piece, image_piece), (slim,))
+        near_kernel, "near", (*numbers, xlow, ylow, xacc, xloss, *r0), (wide, wide, thin, thin, slim)
+    )
+    r2 = exchange(xsend, -2, 2, lambda i: not crosses(i))
+    (r1,) = call(
+        arrived_kernel, "arrived", (text_piece, image_piece, xloss), (slim,), in_specs=[VMEM, VMEM, ANY]
+    )
     r3 = exchange_in_parts(r1, 2, -1, 1)
     xgrad, xloss = call(
         first_kernel, "first", (*numbers, image, text, xlow, xinv, xacc, xloss, r1), (wide, thin)
@@ -240,10 +266,12 @@
     )
     image_grad, text_grad, loss = call(
         last_kernel, "last",
-        (*numbers, image, text, ylow, yinv, yacc, loss, r2, image_grad, text_grad),
+        (*numbers, image, text, ylow, yinv, yacc, loss, r2_across, r2, image_grad, text_grad),
         (wide, wide, jax.ShapeDtypeStruct((rows,), F32)),
-        in_specs=[VMEM] * 9 + [ANY] * 2, out_specs=(ANY, ANY, VMEM), input_output_aliases={9: 0, 10: 1},
-        scratch_shapes=[pltpu.VMEM((rows, width), F32), pltpu.SemaphoreType.DMA((rows // TILE,))],
+        in_specs=[VMEM] * 10 + [ANY] * 2, out_specs=(ANY, ANY, VMEM), input_output_aliases={10: 0, 11: 1},
+        scratch_shapes=[
+            pltpu.VMEM((rows, width), F32), pltpu.SemaphoreType.DMA((rows // TILE,)), pltpu.VMEM((rows, width), BF16),
+        ],
     )
     return loss, image_grad, text_grad
 

time: 76.5 us -> 76.6 us (level)
  starting transfers between devices: 38.1 us -> 33.7 us
  waiting for transfers between devices: 23 us -> 26.3 us
  Pallas kernels: 10.6 us -> 11.7 us
    ppermute x7 -> x8, starting transfers between devices: 38.1 us -> 33.7 us  [exchange(): lax.ppermute(array, AXES, [(i, (i + by) % count) for i, by in steps if by...]
    ppermute x7 -> x8, waiting for transfers between devices: 23 us -> 26.3 us  [exchange(): lax.ppermute(array, AXES, [(i, (i + by) % count) for i, by in steps if by...]
    pallas_call x6 -> x7, Pallas kernels: 10.6 us -> 11.7 us  [call(): pl.pallas_call(kernel, out_shape=outs, compiler_params=PARAMS, cost_estim...]
  transfers between devices with their start and end apart: 7 -> 8, of which waited for: 3 -> 2; matrix products, arithmetic and copies ran while one was open for 0% -> 0% of each run, Pallas kernels for 10% -> 12%
where the time goes in v3:
time: 76.6 us; the launch traced here: 76.2 us
  starting transfers between devices  33.7 us (44%)
  waiting for transfers between devices  26.3 us (34%)
  Pallas kernels  11.7 us (15%)
  local copies, waits for them, and re-layouts  2.37 us (3%)
  between operations  2.11 us (3%)
    ppermute x8, starting transfers between devices, exchange(): lax.ppermute(array, AXES, [(i, (i + by) % count) for i, by in steps if by...  33.7 us
    ppermute x8, waiting for transfers between devices, exchange(): lax.ppermute(array, AXES, [(i, (i + by) % count) for i, by in steps if by...  26.3 us
    pallas_call x7, Pallas kernels, call(): pl.pallas_call(kernel, out_shape=outs, compiler_params=PARAMS, cost_estim...  11.7 us
    unnamed x8, local copies, waits for them, and re-layouts  2.27 us
  transfers between devices with their start and end apart: 8, of which 2 were waited for; matrix products, arithmetic and copies ran while one was open for 0% of the time, Pallas kernels for 12%

profile of v3, /device:TPU:1, one launch (start us, length us, event | category | flops | bytes accessed | tf_op | source)
XLA Modules:
  0.0 76.2 jit_solution(13785714698311992970)
XLA Ops:
  0.6 0.7 collective-permute-start.3
  1.3 8.4 %collective-permute-start.2 = (bf16[512,768]{1,0:T(8,128)(2,1)}, bf16[512,768]{1,0:T(8,128)(2,1)S(1)}, u32[]{:S(2)}, u32[]{:S(2)}) collective-permute-start(bf16[512,768]{1,0:T(8,128)(2,1)} %text.5), channel_id=1, source_target_pairs={{1,3},{3,5},{5,7},{7,9},{9,11},{11,13},{13,15},{15,17},{17,19},{19... | collective-permute-start | bytes 2359304 | tf_op jit(solution)/shard_map/ppermute | solution.py:21
  9.8 0.0 copy-start
  9.8 1.1 %copy-done = bf16[512,768]{1,0:T(8,128)(2,1)S(1)} copy-done((bf16[512,768]{1,0:T(8,128)(2,1)S(1)}, bf16[512,768]{1,0:T(8,128)(2,1)}, u32[]{:S(2)}) %copy-start) | copy-done | bytes 786456
  10.9 0.0 copy-start.2
  10.9 1.1 %copy-done.2 = bf16[512,768]{1,0:T(8,128)(2,1)S(1)} copy-done((bf16[512,768]{1,0:T(8,128)(2,1)S(1)}, bf16[512,768]{1,0:T(8,128)(2,1)}, u32[]{:S(2)}) %copy-start.2) | copy-done | bytes 786456
  12.1 0.7 prepare.1
  12.8 0.1 fusion.1
  12.9 14.7 %collective-permute-start.1 = (bf16[256,768]{1,0:T(8,128)(2,1)S(1)}, bf16[256,768]{1,0:T(8,128)(2,1)S(1)}, u32[]{:S(2)}, u32[]{:S(2)}) collective-permute-start(bf16[256,768]{1,0:T(8,128)(2,1)S(1)} %get-tuple-element.47), channel_id=1, source_target_pairs={{0,1},{1,0},{2,3},{3,2},{4,5},{5,4},{6,7},{7,6},{8,9},{9,8},{10,11... | collective-permute-start | bytes 1179656 | tf_op jit(solution)/shard_map/ppermute | solution.py:21
  27.5 1.9 %collective-permute-start = (bf16[256,768]{1,0:T(8,128)(2,1)S(1)}, bf16[256,768]{1,0:T(8,128)(2,1)S(1)}, u32[]{:S(2)}, u32[]{:S(2)}) collective-permute-start(bf16[256,768]{1,0:T(8,128)(2,1)S(1)} %get-tuple-element.48), channel_id=1, source_target_pairs={{0,1},{1,0},{2,3},{3,2},{4,5},{5,4},{6,7},{7,6},{8,9},{9,8},{10,11... | collective-permute-start | bytes 1179656 | tf_op jit(solution)/shard_map/ppermute | solution.py:21
  30.7 1.6 %local.1 = (f32[512,768]{1,0:T(8,128)S(1)}, f32[512,1]{1,0:T(8,128)S(1)}, bf16[512,768]{1,0:T(8,128)(2,1)S(1)}) custom-call(f32[1,1]{1,0:T(1,128)} %bitcast.2.scale, f32[1,1]{1,0:T(1,128)} %bitcast.7.shift, bf16[512,768]{1,0:T(8,128)(2,1)S(1)} %get-tuple-element.26.xlow, bf16[512,768]{1,0:T(8,128)(2,1)S(1)} %get-tuple-element.24.ylow), custom_call_target="tpu_custom_call" | custom-call | flops 1 | bytes 1 | tf_op jit(solution)/shard_map/local/pallas_call | solution.py:243
  32.4 2.2 %collective-permute-start.6 = (bf16[512,768]{1,0:T(8,128)(2,1)S(1)}, bf16[512,768]{1,0:T(8,128)(2,1)S(1)}, u32[]{:S(2)}, u32[]{:S(2)}) collective-permute-start(bf16[512,768]{1,0:T(8,128)(2,1)S(1)} %get-tuple-element.38), channel_id=1, source_target_pairs={{1,767},{6,8},{9,7},{14,16},{17,15},{22,24},{25,23},{30,32},{33,31... | collective-permute-start | bytes 2359304 | tf_op jit(solution)/shard_map/ppermute | solution.py:21
  34.6 0.0 collective-permute-done.1.refs_1_
  34.6 0.0 collective-permute-done.refs_0_
  34.6 3.3 %near.1 = (f32[512,768]{1,0:T(8,128)S(1)}, f32[512,768]{1,0:T(8,128)S(1)}, f32[512,1]{1,0:T(8,128)S(1)}, f32[512,1]{1,0:T(8,128)S(1)}, bf16[512,768]{1,0:T(8,128)(2,1)S(1)}) custom-call(f32[1,1]{1,0:T(1,128)} %bitcast.3.scale, f32[1,1]{1,0:T(1,128)} %bitcast.8.shift, bf16[512,768]{1,0:T(8,128)(2,1)S(1)} %get-tuple-element.26.xlow, ...), custom_call_target="tpu_custom_call" | custom-call | flops 1 | bytes 1 | tf_op jit(solution)/shard_map/near/pallas_call | solution.py:243
  37.9 1.3 %collective-permute-start.7 = (bf16[512,768]{1,0:T(8,128)(2,1)S(1)}, bf16[512,768]{1,0:T(8,128)(2,1)S(1)}, u32[]{:S(2)}, u32[]{:S(2)}) collective-permute-start(bf16[512,768]{1,0:T(8,128)(2,1)S(1)} %get-tuple-element.39), channel_id=1, source_target_pairs={{0,2},{2,4},{3,1},{4,6},{5,3},{7,5},{8,10},{10,12},{11,9},{12,14},... | collective-permute-start | bytes 2359304 | tf_op jit(solution)/shard_map/ppermute | solution.py:21
  39.2 0.0 collective-permute-done.3.image_piece
  39.2 25.3 %collective-permute-done.2.text_piece = bf16[512,768]{1,0:T(8,128)(2,1)S(1)} collective-permute-done((bf16[512,768]{1,0:T(8,128)(2,1)}, bf16[512,768]{1,0:T(8,128)(2,1)S(1)}, u32[]{:S(2)}, u32[]{:S(2)}) %collective-permute-start.2) | collective-permute-done | bytes 786464 | tf_op jit(solution)/shard_map/ppermute | solution.py:21
  64.5 0.0 copy-start.1
  64.5 0.4 arrived.1.low
  64.9 0.1 fusion
  65.0 2.1 %collective-permute-start.5 = (bf16[256,768]{1,0:T(8,128)(2,1)S(1)}, bf16[256,768]{1,0:T(8,128)(2,1)S(1)}, u32[]{:S(2)}, u32[]{:S(2)}) collective-permute-start(bf16[256,768]{1,0:T(8,128)(2,1)S(1)} %get-tuple-element.45), channel_id=1, source_target_pairs={{0,1},{1,0},{2,3},{3,2},{4,5},{5,4},{6,7},{7,6},{8,9},{9,8},{10,11... | collective-permute-start | bytes 1179656 | tf_op jit(solution)/shard_map/ppermute | solution.py:21
  67.0 2.4 %collective-permute-start.4 = (bf16[256,768]{1,0:T(8,128)(2,1)S(1)}, bf16[256,768]{1,0:T(8,128)(2,1)S(1)}, u32[]{:S(2)}, u32[]{:S(2)}) collective-permute-start(bf16[256,768]{1,0:T(8,128)(2,1)S(1)} %get-tuple-element.46), channel_id=1, source_target_pairs={{0,1},{1,0},{2,3},{3,2},{4,5},{5,4},{6,7},{7,6},{8,9},{9,8},{10,11... | collective-permute-start | bytes 1179656 | tf_op jit(solution)/shard_map/ppermute | solution.py:21
  69.4 0.0 copy-done.1
  69.4 0.0 copy-done.3
  69.5 1.6 %first.1 = (f32[512,768]{1,0:T(8,128)S(1)}, f32[512,1]{1,0:T(8,128)S(1)}) custom-call(f32[1,1]{1,0:T(1,128)} %bitcast.4.scale, f32[1,1]{1,0:T(1,128)} %bitcast.9.shift, bf16[512,768]{1,0:T(8,128)(2,1)S(1)} %copy-done.1, bf16[512,768]{1,0:T(8,128)(2,1)S(1)} %copy-done.3, bf16[512,768]{1,0:T(8,128)(2,1)S(1)} %get-tuple-element.26.xlow, ...), custom_call_target="tpu_custom_call" | custom-call | flops 1 | bytes 1 | tf_op jit(solution)/shard_map/first/pallas_call | solution.py:243
  71.1 0.0 collective-permute-done.5.refs_1_
  71.1 0.0 collective-permute-done.4.refs_0_
  71.1 1.2 %second.1 = (f32[512,768]{1,0:T(8,128)S(1)}, f32[512,1]{1,0:T(8,128)S(1)}, f32[512,768]{1,0:T(8,128)}, f32[512,768]{1,0:T(8,128)}) custom-call(f32[1,1]{1,0:T(1,128)} %bitcast.5.scale, f32[1,1]{1,0:T(1,128)} %bitcast.10.shift, bf16[512,768]{1,0:T(8,128)(2,1)S(1)} %get-tuple-element.24.ylow, f32[512,768]{1,0:T(8,128)S(1)} %get-tuple-element.29.yacc_in, ...), custom_call_target="tpu_custom_call" | custom-call | flops 1 | bytes 1 | tf_op jit(solution)/shard_map/second/pallas_call | solution.py:243
  72.3 1.0 %collective-permute-done.6.r2_across = bf16[512,768]{1,0:T(8,128)(2,1)S(1)} collective-permute-done((bf16[512,768]{1,0:T(8,128)(2,1)S(1)}, bf16[512,768]{1,0:T(8,128)(2,1)S(1)}, u32[]{:S(2)}, u32[]{:S(2)}) %collective-permute-start.6) | collective-permute-done | bytes 786464 | tf_op jit(solution)/shard_map/ppermute | solution.py:21
  73.3 0.0 collective-permute-done.7.r2
  73.3 2.9 %last.1 = (f32[512,768]{1,0:T(8,128)}, f32[512,768]{1,0:T(8,128)}, f32[512]{0:T(512)}) custom-call(f32[1,1]{1,0:T(1,128)} %bitcast.6.scale, f32[1,1]{1,0:T(1,128)} %bitcast.11.shift, bf16[512,768]{1,0:T(8,128)(2,1)S(1)} %copy-done.1, bf16[512,768]{1,0:T(8,128)(2,1)S(1)} %copy-done.3, ...), custom_call_target="tpu_custom_call", output_to_operand_aliasing={{0}: (10, {}), {1}: (11, {})} | custom-call | flops 1 | bytes 1 | tf_op jit(solution)/shard_map/last/pallas_call | solution.py:243
  (1 shorter events, 0.0 us)
Async XLA Ops:
  0.6 38.6 %collective-permute-start.3 = (bf16[512,768]{1,0:T(8,128)(2,1)}, bf16[512,768]{1,0:T(8,128)(2,1)S(1)}, u32[]{:S(2)}, u32[]{:S(2)}) collective-permute-start(bf16[512,768]{1,0:T(8,128)(2,1)} %image.5), channel_id=1, source_target_pairs={{0,766},{2,0},{4,2},{6,4},{8,6},{10,8},{12,10},{14,12},{16,14},{18... | collective-permute-start | bytes 2359304 | tf_op jit(solution)/shard_map/ppermute | solution.py:21
  1.3 63.2 %collective-permute-start.2 = (bf16[512,768]{1,0:T(8,128)(2,1)}, bf16[512,768]{1,0:T(8,128)(2,1)S(1)}, u32[]{:S(2)}, u32[]{:S(2)}) collective-permute-start(bf16[512,768]{1,0:T(8,128)(2,1)} %text.5), channel_id=1, source_target_pairs={{1,3},{3,5},{5,7},{7,9},{9,11},{11,13},{13,15},{15,17},{17,19},{19... | collective-permute-start | bytes 2359304 | tf_op jit(solution)/shard_map/ppermute | solution.py:21
  9.8 1.1 %copy-start = (bf16[512,768]{1,0:T(8,128)(2,1)S(1)}, bf16[512,768]{1,0:T(8,128)(2,1)}, u32[]{:S(2)}) copy-start(bf16[512,768]{1,0:T(8,128)(2,1)} %image.5) | copy-start | bytes 2359300
  10.9 1.1 %copy-start.2 = (bf16[512,768]{1,0:T(8,128)(2,1)S(1)}, bf16[512,768]{1,0:T(8,128)(2,1)}, u32[]{:S(2)}) copy-start(bf16[512,768]{1,0:T(8,128)(2,1)} %text.5) | copy-start | bytes 2359300
  12.9 21.7 %collective-permute-start.1 = (bf16[256,768]{1,0:T(8,128)(2,1)S(1)}, bf16[256,768]{1,0:T(8,128)(2,1)S(1)}, u32[]{:S(2)}, u32[]{:S(2)}) collective-permute-start(bf16[256,768]{1,0:T(8,128)(2,1)S(1)} %get-tuple-element.47), channel_id=1, source_target_pairs={{0,1},{1,0},{2,3},{3,2},{4,5},{5,4},{6,7},{7,6},{8,9},{9,8},{10,11... | collective-permute-start | bytes 1179656 | tf_op jit(solution)/shard_map/ppermute | solution.py:21
  27.5 7.1 %collective-permute-start = (bf16[256,768]{1,0:T(8,128)(2,1)S(1)}, bf16[256,768]{1,0:T(8,128)(2,1)S(1)}, u32[]{:S(2)}, u32[]{:S(2)}) collective-permute-start(bf16[256,768]{1,0:T(8,128)(2,1)S(1)} %get-tuple-element.48), channel_id=1, source_target_pairs={{0,1},{1,0},{2,3},{3,2},{4,5},{5,4},{6,7},{7,6},{8,9},{9,8},{10,11... | collective-permute-start | bytes 1179656 | tf_op jit(solution)/shard_map/ppermute | solution.py:21
  32.4 40.9 %collective-permute-start.6 = (bf16[512,768]{1,0:T(8,128)(2,1)S(1)}, bf16[512,768]{1,0:T(8,128)(2,1)S(1)}, u32[]{:S(2)}, u32[]{:S(2)}) collective-permute-start(bf16[512,768]{1,0:T(8,128)(2,1)S(1)} %get-tuple-element.38), channel_id=1, source_target_pairs={{1,767},{6,8},{9,7},{14,16},{17,15},{22,24},{25,23},{30,32},{33,31... | collective-permute-start | bytes 2359304 | tf_op jit(solution)/shard_map/ppermute | solution.py:21
  37.9 35.3 %collective-permute-start.7 = (bf16[512,768]{1,0:T(8,128)(2,1)S(1)}, bf16[512,768]{1,0:T(8,128)(2,1)S(1)}, u32[]{:S(2)}, u32[]{:S(2)}) collective-permute-start(bf16[512,768]{1,0:T(8,128)(2,1)S(1)} %get-tuple-element.39), channel_id=1, source_target_pairs={{0,2},{2,4},{3,1},{4,6},{5,3},{7,5},{8,10},{10,12},{11,9},{12,14},... | collective-permute-start | bytes 2359304 | tf_op jit(solution)/shard_map/ppermute | solution.py:21
  64.5 4.9 %copy-start.1 = (bf16[512,768]{1,0:T(8,128)(2,1)S(1)}, bf16[512,768]{1,0:T(8,128)(2,1)}, u32[]{:S(2)}) copy-start(bf16[512,768]{1,0:T(8,128)(2,1)} %image.5) | copy-start | bytes 2359300
  64.5 4.9 %copy-start.3 = (bf16[512,768]{1,0:T(8,128)(2,1)S(1)}, bf16[512,768]{1,0:T(8,128)(2,1)}, u32[]{:S(2)}) copy-start(bf16[512,768]{1,0:T(8,128)(2,1)} %text.5) | copy-start | bytes 2359300
  65.0 6.1 %collective-permute-start.5 = (bf16[256,768]{1,0:T(8,128)(2,1)S(1)}, bf16[256,768]{1,0:T(8,128)(2,1)S(1)}, u32[]{:S(2)}, u32[]{:S(2)}) collective-permute-start(bf16[256,768]{1,0:T(8,128)(2,1)S(1)} %get-tuple-element.45), channel_id=1, source_target_pairs={{0,1},{1,0},{2,3},{3,2},{4,5},{5,4},{6,7},{7,6},{8,9},{9,8},{10,11... | collective-permute-start | bytes 1179656 | tf_op jit(solution)/shard_map/ppermute | solution.py:21
  67.0 4.1 %collective-permute-start.4 = (bf16[256,768]{1,0:T(8,128)(2,1)S(1)}, bf16[256,768]{1,0:T(8,128)(2,1)S(1)}, u32[]{:S(2)}, u32[]{:S(2)}) collective-permute-start(bf16[256,768]{1,0:T(8,128)(2,1)S(1)} %get-tuple-element.46), channel_id=1, source_target_pairs={{0,1},{1,0},{2,3},{3,2},{4,5},{5,4},{6,7},{7,6},{8,9},{9,8},{10,11... | collective-permute-start | bytes 1179656 | tf_op jit(solution)/shard_map/ppermute | solution.py:21

commit v4 on v3

--- a/solution.py
+++ b/solution.py
@@ -150,7 +150,7 @@
 
 
 def second_kernel(scale, shift, ylow, yacc_in, yloss_in, xloss, xgrad, *refs):
-    pieces, (yacc, loss, image_grad, text_grad, sem) = refs[:-5], refs[-5:]
+    pieces, (yacc, loss, mean, image_grad, text_grad, sem) = refs[:-6], refs[-6:]
     temper, offset = scale[...], shift[...]
     odd = is_odd()
 
@@ -169,7 +169,8 @@
                 coef, plus = terms(tile)
                 total += plus
                 acc += weighted(coef, piece[...])
-            loss[at, :] = jnp.where(odd, xloss[at, :], total)
+            loss[at, :] = total
+            mean[at] = jnp.sum(xloss[at, :], axis=1) * (1.0 / ylow.shape[0])
             yacc[at, :] = acc
         copy.wait()
 
@@ -183,7 +184,7 @@
 
 
 def last_kernel(
-    scale, shift, image, text, ylow, yinv, yacc, loss_in, r2_across, r2, image_in, text_in,
+    scale, shift, image, text, ylow, yinv, yacc, loss_in, mean, r2_across, r2, image_in, text_in,
     image_grad, text_grad, loss, ygrad, sems, low,
 ):
     del image_in, text_in
@@ -210,8 +211,10 @@
             acc = yacc[at, :] + weighted(coef, low[...])
             ygrad[at, :] = finished(acc, raw[at, :].astype(F32), yinv[at, :], temper)
             copy.start()
-            total = loss_in[at, :] + plus if counted else loss_in[at, :]
-            loss[at] = jnp.sum(total, axis=1) * (1.0 / rows)
+            if counted:
+                loss[at] = jnp.sum(loss_in[at, :] + plus, axis=1) * (1.0 / rows)
+            else:
+                loss[at] = mean[at]
         for copy in copies:
             copy.wait()
 
@@ -236,6 +239,7 @@
     wide = jax.ShapeDtypeStruct((rows, width), F32)
     slim = jax.ShapeDtypeStruct((rows, width), BF16)
     thin = jax.ShapeDtypeStruct((rows, 1), F32)
+    flat = jax.ShapeDtypeStruct((rows,), F32)
 
     def call(kernel, name, inputs, outs, **more):
         specs = dict(out_specs=(VMEM,) * len(outs), in_specs=[VMEM] * len(inputs))
@@ -260,15 +264,15 @@
     xgrad, xloss = call(
         first_kernel, "first", (*numbers, image, text, xlow, xinv, xacc, xloss, r1), (wide, thin)
     )
-    yacc, loss, image_grad, text_grad = call(
-        second_kernel, "second", (*numbers, ylow, yacc, yloss, xloss, xgrad, *r3), (wide, thin, wide, wide),
-        out_specs=(VMEM, VMEM, ANY, ANY), scratch_shapes=[pltpu.SemaphoreType.DMA],
+    yacc, loss, mean, image_grad, text_grad = call(
+        second_kernel, "second", (*numbers, ylow, yacc, yloss, xloss, xgrad, *r3), (wide, thin, flat, wide, wide),
+        out_specs=(VMEM, VMEM, VMEM, ANY, ANY), scratch_shapes=[pltpu.SemaphoreType.DMA],
     )
     image_grad, text_grad, loss = call(
         last_kernel, "last",
-        (*numbers, image, text, ylow, yinv, yacc, loss, r2_across, r2, image_grad, text_grad),
-        (wide, wide, jax.ShapeDtypeStruct((rows,), F32)),
-        in_specs=[VMEM] * 10 + [ANY] * 2, out_specs=(ANY, ANY, VMEM), input_output_aliases={10: 0, 11: 1},
+        (*numbers, image, text, ylow, yinv, yacc, loss, mean, r2_across, r2, image_grad, text_grad),
+        (wide, wide, flat),
+        in_specs=[VMEM] * 11 + [ANY] * 2, out_specs=(ANY, ANY, VMEM), input_output_aliases={11: 0, 12: 1},
         scratch_shapes=[
             pltpu.VMEM((rows, width), F32), pltpu.SemaphoreType.DMA((rows // TILE,)), pltpu.VMEM((rows, width), BF16),
         ],

time: 76.6 us -> 76.6 us (level)
  no operation moved by 1% of the time
where the time goes in v4:
time: 76.6 us; the launch traced here: 76.2 us
  starting transfers between devices  33.7 us (44%)
  waiting for transfers between devices  26 us (34%)
  Pallas kernels  12 us (16%)
  local copies, waits for them, and re-layouts  2.37 us (3%)
  between operations  2.11 us (3%)
    ppermute x8, starting transfers between devices, exchange(): lax.ppermute(array, AXES, [(i, (i + by) % count) for i, by in steps if by...  33.7 us
    ppermute x8, waiting for transfers between devices, exchange(): lax.ppermute(array, AXES, [(i, (i + by) % count) for i, by in steps if by...  26 us
    pallas_call x7, Pallas kernels, call(): pl.pallas_call(kernel, out_shape=outs, compiler_params=PARAMS, cost_estim...  12 us
    unnamed x8, local copies, waits for them, and re-layouts  2.27 us
  transfers between devices with their start and end apart: 8, of which 2 were waited for; matrix products, arithmetic and copies ran while one was open for 0% of the time, Pallas kernels for 12%

profile of v4, /device:TPU:1, one launch (start us, length us, event | category | flops | bytes accessed | tf_op | source)
XLA Modules:
  0.0 76.2 jit_solution(13079347476805164342)
XLA Ops:
  0.6 0.7 collective-permute-start.3
  1.3 8.4 %collective-permute-start.2 = (bf16[512,768]{1,0:T(8,128)(2,1)}, bf16[512,768]{1,0:T(8,128)(2,1)S(1)}, u32[]{:S(2)}, u32[]{:S(2)}) collective-permute-start(bf16[512,768]{1,0:T(8,128)(2,1)} %text.5), channel_id=1, source_target_pairs={{1,3},{3,5},{5,7},{7,9},{9,11},{11,13},{13,15},{15,17},{17,19},{19... | collective-permute-start | bytes 2359304 | tf_op jit(solution)/shard_map/ppermute | solution.py:21
  9.8 0.0 copy-start
  9.8 1.1 %copy-done = bf16[512,768]{1,0:T(8,128)(2,1)S(1)} copy-done((bf16[512,768]{1,0:T(8,128)(2,1)S(1)}, bf16[512,768]{1,0:T(8,128)(2,1)}, u32[]{:S(2)}) %copy-start) | copy-done | bytes 786456
  10.9 0.0 copy-start.2
  10.9 1.1 %copy-done.2 = bf16[512,768]{1,0:T(8,128)(2,1)S(1)} copy-done((bf16[512,768]{1,0:T(8,128)(2,1)S(1)}, bf16[512,768]{1,0:T(8,128)(2,1)}, u32[]{:S(2)}) %copy-start.2) | copy-done | bytes 786456
  12.1 0.7 prepare.1
  12.8 0.1 fusion.1
  12.9 14.7 %collective-permute-start.1 = (bf16[256,768]{1,0:T(8,128)(2,1)S(1)}, bf16[256,768]{1,0:T(8,128)(2,1)S(1)}, u32[]{:S(2)}, u32[]{:S(2)}) collective-permute-start(bf16[256,768]{1,0:T(8,128)(2,1)S(1)} %get-tuple-element.49), channel_id=1, source_target_pairs={{0,1},{1,0},{2,3},{3,2},{4,5},{5,4},{6,7},{7,6},{8,9},{9,8},{10,11... | collective-permute-start | bytes 1179656 | tf_op jit(solution)/shard_map/ppermute | solution.py:21
  27.5 1.9 %collective-permute-start = (bf16[256,768]{1,0:T(8,128)(2,1)S(1)}, bf16[256,768]{1,0:T(8,128)(2,1)S(1)}, u32[]{:S(2)}, u32[]{:S(2)}) collective-permute-start(bf16[256,768]{1,0:T(8,128)(2,1)S(1)} %get-tuple-element.50), channel_id=1, source_target_pairs={{0,1},{1,0},{2,3},{3,2},{4,5},{5,4},{6,7},{7,6},{8,9},{9,8},{10,11... | collective-permute-start | bytes 1179656 | tf_op jit(solution)/shard_map/ppermute | solution.py:21
  30.7 1.6 %local.1 = (f32[512,768]{1,0:T(8,128)S(1)}, f32[512,1]{1,0:T(8,128)S(1)}, bf16[512,768]{1,0:T(8,128)(2,1)S(1)}) custom-call(f32[1,1]{1,0:T(1,128)} %bitcast.2.scale, f32[1,1]{1,0:T(1,128)} %bitcast.7.shift, bf16[512,768]{1,0:T(8,128)(2,1)S(1)} %get-tuple-element.27.xlow, bf16[512,768]{1,0:T(8,128)(2,1)S(1)} %get-tuple-element.25.ylow), custom_call_target="tpu_custom_call" | custom-call | flops 1 | bytes 1 | tf_op jit(solution)/shard_map/local/pallas_call | solution.py:247
  32.4 2.2 %collective-permute-start.6 = (bf16[512,768]{1,0:T(8,128)(2,1)S(1)}, bf16[512,768]{1,0:T(8,128)(2,1)S(1)}, u32[]{:S(2)}, u32[]{:S(2)}) collective-permute-start(bf16[512,768]{1,0:T(8,128)(2,1)S(1)} %get-tuple-element.40), channel_id=1, source_target_pairs={{1,767},{6,8},{9,7},{14,16},{17,15},{22,24},{25,23},{30,32},{33,31... | collective-permute-start | bytes 2359304 | tf_op jit(solution)/shard_map/ppermute | solution.py:21
  34.6 0.0 collective-permute-done.1.refs_1_
  34.6 0.0 collective-permute-done.refs_0_
  34.6 3.3 %near.1 = (f32[512,768]{1,0:T(8,128)S(1)}, f32[512,768]{1,0:T(8,128)S(1)}, f32[512,1]{1,0:T(8,128)S(1)}, f32[512,1]{1,0:T(8,128)S(1)}, bf16[512,768]{1,0:T(8,128)(2,1)S(1)}) custom-call(f32[1,1]{1,0:T(1,128)} %bitcast.3.scale, f32[1,1]{1,0:T(1,128)} %bitcast.8.shift, bf16[512,768]{1,0:T(8,128)(2,1)S(1)} %get-tuple-element.27.xlow, ...), custom_call_target="tpu_custom_call" | custom-call | flops 1 | bytes 1 | tf_op jit(solution)/shard_map/near/pallas_call | solution.py:247
  37.9 1.3 %collective-permute-start.7 = (bf16[512,768]{1,0:T(8,128)(2,1)S(1)}, bf16[512,768]{1,0:T(8,128)(2,1)S(1)}, u32[]{:S(2)}, u32[]{:S(2)}) collective-permute-start(bf16[512,768]{1,0:T(8,128)(2,1)S(1)} %get-tuple-element.41), channel_id=1, source_target_pairs={{0,2},{2,4},{3,1},{4,6},{5,3},{7,5},{8,10},{10,12},{11,9},{12,14},... | collective-permute-start | bytes 2359304 | tf_op jit(solution)/shard_map/ppermute | solution.py:21
  39.2 0.0 collective-permute-done.3.image_piece
  39.2 25.3 %collective-permute-done.2.text_piece = bf16[512,768]{1,0:T(8,128)(2,1)S(1)} collective-permute-done((bf16[512,768]{1,0:T(8,128)(2,1)}, bf16[512,768]{1,0:T(8,128)(2,1)S(1)}, u32[]{:S(2)}, u32[]{:S(2)}) %collective-permute-start.2) | collective-permute-done | bytes 786464 | tf_op jit(solution)/shard_map/ppermute | solution.py:21
  64.5 0.0 copy-start.1
  64.5 0.4 arrived.1.low
  64.9 0.1 fusion
  65.0 2.1 %collective-permute-start.5 = (bf16[256,768]{1,0:T(8,128)(2,1)S(1)}, bf16[256,768]{1,0:T(8,128)(2,1)S(1)}, u32[]{:S(2)}, u32[]{:S(2)}) collective-permute-start(bf16[256,768]{1,0:T(8,128)(2,1)S(1)} %get-tuple-element.47), channel_id=1, source_target_pairs={{0,1},{1,0},{2,3},{3,2},{4,5},{5,4},{6,7},{7,6},{8,9},{9,8},{10,11... | collective-permute-start | bytes 1179656 | tf_op jit(solution)/shard_map/ppermute | solution.py:21
  67.0 2.4 %collective-permute-start.4 = (bf16[256,768]{1,0:T(8,128)(2,1)S(1)}, bf16[256,768]{1,0:T(8,128)(2,1)S(1)}, u32[]{:S(2)}, u32[]{:S(2)}) collective-permute-start(bf16[256,768]{1,0:T(8,128)(2,1)S(1)} %get-tuple-element.48), channel_id=1, source_target_pairs={{0,1},{1,0},{2,3},{3,2},{4,5},{5,4},{6,7},{7,6},{8,9},{9,8},{10,11... | collective-permute-start | bytes 1179656 | tf_op jit(solution)/shard_map/ppermute | solution.py:21
  69.4 0.0 copy-done.1
  69.4 0.0 copy-done.3
  69.5 1.6 %first.1 = (f32[512,768]{1,0:T(8,128)S(1)}, f32[512,1]{1,0:T(8,128)S(1)}) custom-call(f32[1,1]{1,0:T(1,128)} %bitcast.4.scale, f32[1,1]{1,0:T(1,128)} %bitcast.9.shift, bf16[512,768]{1,0:T(8,128)(2,1)S(1)} %copy-done.1, bf16[512,768]{1,0:T(8,128)(2,1)S(1)} %copy-done.3, bf16[512,768]{1,0:T(8,128)(2,1)S(1)} %get-tuple-element.27.xlow, ...), custom_call_target="tpu_custom_call" | custom-call | flops 1 | bytes 1 | tf_op jit(solution)/shard_map/first/pallas_call | solution.py:247
  71.1 0.0 collective-permute-done.5.refs_1_
  71.1 0.0 collective-permute-done.4.refs_0_
  71.1 1.5 %second.1 = (f32[512,768]{1,0:T(8,128)S(1)}, f32[512,1]{1,0:T(8,128)S(1)}, f32[512]{0:T(512)S(1)}, f32[512,768]{1,0:T(8,128)}, f32[512,768]{1,0:T(8,128)}) custom-call(f32[1,1]{1,0:T(1,128)} %bitcast.5.scale, f32[1,1]{1,0:T(1,128)} %bitcast.10.shift, bf16[512,768]{1,0:T(8,128)(2,1)S(1)} %get-tuple-element.25.ylow, f32[512,768]{1,0:T(8,128)S(1)} %get-tuple-element.30.yacc_in, ...), custom_call_target="tpu_custom_call" | custom-call | flops 1 | bytes 1 | tf_op jit(solution)/shard_map/second/pallas_call | solution.py:247
  72.6 0.7 collective-permute-done.6.r2_across
  73.3 0.0 collective-permute-done.7.r2
  73.3 2.9 %last.1 = (f32[512,768]{1,0:T(8,128)}, f32[512,768]{1,0:T(8,128)}, f32[512]{0:T(512)}) custom-call(f32[1,1]{1,0:T(1,128)} %bitcast.6.scale, f32[1,1]{1,0:T(1,128)} %bitcast.11.shift, bf16[512,768]{1,0:T(8,128)(2,1)S(1)} %copy-done.1, bf16[512,768]{1,0:T(8,128)(2,1)S(1)} %copy-done.3, ...), custom_call_target="tpu_custom_call", output_to_operand_aliasing={{0}: (11, {}), {1}: (12, {})} | custom-call | flops 1 | bytes 1 | tf_op jit(solution)/shard_map/last/pallas_call | solution.py:247
  (1 shorter events, 0.0 us)
Async XLA Ops:
  0.6 38.6 %collective-permute-start.3 = (bf16[512,768]{1,0:T(8,128)(2,1)}, bf16[512,768]{1,0:T(8,128)(2,1)S(1)}, u32[]{:S(2)}, u32[]{:S(2)}) collective-permute-start(bf16[512,768]{1,0:T(8,128)(2,1)} %image.5), channel_id=1, source_target_pairs={{0,766},{2,0},{4,2},{6,4},{8,6},{10,8},{12,10},{14,12},{16,14},{18... | collective-permute-start | bytes 2359304 | tf_op jit(solution)/shard_map/ppermute | solution.py:21
  1.3 63.2 %collective-permute-start.2 = (bf16[512,768]{1,0:T(8,128)(2,1)}, bf16[512,768]{1,0:T(8,128)(2,1)S(1)}, u32[]{:S(2)}, u32[]{:S(2)}) collective-permute-start(bf16[512,768]{1,0:T(8,128)(2,1)} %text.5), channel_id=1, source_target_pairs={{1,3},{3,5},{5,7},{7,9},{9,11},{11,13},{13,15},{15,17},{17,19},{19... | collective-permute-start | bytes 2359304 | tf_op jit(solution)/shard_map/ppermute | solution.py:21
  9.8 1.1 %copy-start = (bf16[512,768]{1,0:T(8,128)(2,1)S(1)}, bf16[512,768]{1,0:T(8,128)(2,1)}, u32[]{:S(2)}) copy-start(bf16[512,768]{1,0:T(8,128)(2,1)} %image.5) | copy-start | bytes 2359300
  10.9 1.1 %copy-start.2 = (bf16[512,768]{1,0:T(8,128)(2,1)S(1)}, bf16[512,768]{1,0:T(8,128)(2,1)}, u32[]{:S(2)}) copy-start(bf16[512,768]{1,0:T(8,128)(2,1)} %text.5) | copy-start | bytes 2359300
  12.9 21.7 %collective-permute-start.1 = (bf16[256,768]{1,0:T(8,128)(2,1)S(1)}, bf16[256,768]{1,0:T(8,128)(2,1)S(1)}, u32[]{:S(2)}, u32[]{:S(2)}) collective-permute-start(bf16[256,768]{1,0:T(8,128)(2,1)S(1)} %get-tuple-element.49), channel_id=1, source_target_pairs={{0,1},{1,0},{2,3},{3,2},{4,5},{5,4},{6,7},{7,6},{8,9},{9,8},{10,11... | collective-permute-start | bytes 1179656 | tf_op jit(solution)/shard_map/ppermute | solution.py:21
  27.5 7.1 %collective-permute-start = (bf16[256,768]{1,0:T(8,128)(2,1)S(1)}, bf16[256,768]{1,0:T(8,128)(2,1)S(1)}, u32[]{:S(2)}, u32[]{:S(2)}) collective-permute-start(bf16[256,768]{1,0:T(8,128)(2,1)S(1)} %get-tuple-element.50), channel_id=1, source_target_pairs={{0,1},{1,0},{2,3},{3,2},{4,5},{5,4},{6,7},{7,6},{8,9},{9,8},{10,11... | collective-permute-start | bytes 1179656 | tf_op jit(solution)/shard_map/ppermute | solution.py:21
  32.4 40.9 %collective-permute-start.6 = (bf16[512,768]{1,0:T(8,128)(2,1)S(1)}, bf16[512,768]{1,0:T(8,128)(2,1)S(1)}, u32[]{:S(2)}, u32[]{:S(2)}) collective-permute-start(bf16[512,768]{1,0:T(8,128)(2,1)S(1)} %get-tuple-element.40), channel_id=1, source_target_pairs={{1,767},{6,8},{9,7},{14,16},{17,15},{22,24},{25,23},{30,32},{33,31... | collective-permute-start | bytes 2359304 | tf_op jit(solution)/shard_map/ppermute | solution.py:21
  37.9 35.3 %collective-permute-start.7 = (bf16[512,768]{1,0:T(8,128)(2,1)S(1)}, bf16[512,768]{1,0:T(8,128)(2,1)S(1)}, u32[]{:S(2)}, u32[]{:S(2)}) collective-permute-start(bf16[512,768]{1,0:T(8,128)(2,1)S(1)} %get-tuple-element.41), channel_id=1, source_target_pairs={{0,2},{2,4},{3,1},{4,6},{5,3},{7,5},{8,10},{10,12},{11,9},{12,14},... | collective-permute-start | bytes 2359304 | tf_op jit(solution)/shard_map/ppermute | solution.py:21
  64.5 4.9 %copy-start.1 = (bf16[512,768]{1,0:T(8,128)(2,1)S(1)}, bf16[512,768]{1,0:T(8,128)(2,1)}, u32[]{:S(2)}) copy-start(bf16[512,768]{1,0:T(8,128)(2,1)} %image.5) | copy-start | bytes 2359300
  64.5 4.9 %copy-start.3 = (bf16[512,768]{1,0:T(8,128)(2,1)S(1)}, bf16[512,768]{1,0:T(8,128)(2,1)}, u32[]{:S(2)}) copy-start(bf16[512,768]{1,0:T(8,128)(2,1)} %text.5) | copy-start | bytes 2359300
  65.0 6.1 %collective-permute-start.5 = (bf16[256,768]{1,0:T(8,128)(2,1)S(1)}, bf16[256,768]{1,0:T(8,128)(2,1)S(1)}, u32[]{:S(2)}, u32[]{:S(2)}) collective-permute-start(bf16[256,768]{1,0:T(8,128)(2,1)S(1)} %get-tuple-element.47), channel_id=1, source_target_pairs={{0,1},{1,0},{2,3},{3,2},{4,5},{5,4},{6,7},{7,6},{8,9},{9,8},{10,11... | collective-permute-start | bytes 1179656 | tf_op jit(solution)/shard_map/ppermute | solution.py:21
  67.0 4.1 %collective-permute-start.4 = (bf16[256,768]{1,0:T(8,128)(2,1)S(1)}, bf16[256,768]{1,0:T(8,128)(2,1)S(1)}, u32[]{:S(2)}, u32[]{:S(2)}) collective-permute-start(bf16[256,768]{1,0:T(8,128)(2,1)S(1)} %get-tuple-element.48), channel_id=1, source_target_pairs={{0,1},{1,0},{2,3},{3,2},{4,5},{5,4},{6,7},{7,6},{8,9},{9,8},{10,11... | collective-permute-start | bytes 1179656 | tf_op jit(solution)/shard_map/ppermute | solution.py:21
